TPU v7x, 32 devices: a whole 2x2x4 slice. The times are simulated.
32 devices in a mesh: req: 8 (over y, x, core), head: 4 (over z).
Axes of the slice: x: 2, y: 2, z: 4, core: 2. Of those that a mesh axis runs over, the one named last changes fastest.
Arguments:
- hidden_in: bfloat16 [2048, 2048], P(('req', 'head')), may hold values from -6 to 6
- segment_ids: int32 [8, 256], P('req', 'head'), may hold values from 0 to 3, never falling along the last dimension, each value on 1 to 128 neighbouring positions
- attn_routes: int32 [2048, 2], P(('req', 'head')), may hold values from 0 to 7, all different within a row; in each aligned block of 256 rows (0 to 255, 256 to 511, ...) at most 96 rows name the same one
- ffn_routes: int32 [2048, 2], P(('req', 'head')), may hold values from 0 to 7, all different within a row; in each aligned block of 64 rows (0 to 63, 64 to 127, ...) at most 24 rows name the same one
- attn_gain: float32 [2048], replicated, may hold values from 0.1 to 1.9
- attn_router: float32 [2048, 8], replicated, may hold values from -0.125 to 0.125
- w_query: bfloat16 [8, 2048, 2048], P(None, None, 'head'), may hold values from -1 to 1
- w_key: bfloat16 [2048, 2048], P(None, 'head'), may hold values from -32 to 32
- w_value: bfloat16 [2048, 2048], P(None, 'head'), may hold values from -0.125 to 0.125
- w_out: bfloat16 [8, 2048, 2048], P(None, 'head'), may hold values from -0.125 to 0.125
- ffn_gain: float32 [2048], replicated, may hold values from 0.1 to 1.9
- ffn_router: float32 [2048, 8], replicated, may hold values from -0.125 to 0.125
- w_gate_up: bfloat16 [8, 2048, 2, 5632], P('head', None, None, 'req'), may hold values from -0.125 to 0.125
- w_down: bfloat16 [8, 5632, 2048], P('head', 'req'), may hold values from -0.078125 to 0.078125
Outputs:
- layer_out: bfloat16 [2048, 2048], P(('req', 'head'))
Inputs may be any that keep to these rules, and one draw needn't show every extreme that they name: `segment_ids`: within each row segment numbers never fall; each segment has 1 to 128 tokens. `attn_routes`: each token names two different experts; in each aligned block of 256 rows no expert is named by more than 96 rows. `ffn_routes`: each token names two different experts; in each aligned block of 64 rows (the rows of one device) no expert is named by more than 24 rows.
All inputs are finite; a program needn't handle non-finite values.
Results may differ from a plain program's by a relative error of at most 0.015.
Values may be sent and summed in bfloat16 or wider, within the bound.
A program may use at most 128 MiB of HBM per device.

v0:
```python
import jax
import jax.numpy as jnp
from jax import lax
from jax.sharding import PartitionSpec as P

D = 2048
HD = 128
E_ATT = 8
E_FF = 8


EPSILON = 1e-06
ROPE_BASE = 10000.0


def rms_norm(values, gain_vector):
    widened = values.astype(jnp.float32)
    inverse_rms = lax.rsqrt(jnp.mean(widened * widened, axis=-1, keepdims=True) + EPSILON)
    return (widened * inverse_rms * gain_vector).astype(jnp.bfloat16)


def pair_gates(normed, router, routes):
    logits = jnp.dot(normed.astype(jnp.float32), router, precision=lax.Precision.HIGHEST)
    picked = jnp.take_along_axis(logits, routes, axis=1)
    first_weight = jax.nn.sigmoid(picked[:, 0] - picked[:, 1])
    second_weight = jax.nn.sigmoid(picked[:, 1] - picked[:, 0])
    return jnp.stack([first_weight, second_weight], axis=1)


def positions(segment_row):
    earlier = (segment_row[None, :] < segment_row[:, None]).astype(jnp.int32)
    return jnp.arange(segment_row.shape[0], dtype=jnp.int32) - jnp.sum(earlier, axis=1)


def rotary(values, token_place):
    half_width = values.shape[-1] // 2
    inverse = ROPE_BASE ** (-jnp.arange(half_width, dtype=jnp.float32) / half_width)
    shaped = token_place.astype(jnp.float32).reshape((-1,) + (1,) * (values.ndim - 2) + (1,))
    angles = shaped * inverse
    cosine = jnp.cos(angles)
    sines = jnp.sin(angles)
    lower_half = values[..., :half_width]
    upper_half = values[..., half_width:]
    return jnp.concatenate(
        [lower_half * cosine - upper_half * sines, upper_half * cosine + lower_half * sines],
        axis=-1,
    )


def slot_ranks(experts_flat, expert_count):
    onehot = (experts_flat[:, None] == jnp.arange(expert_count, dtype=jnp.int32)[None, :]).astype(
        jnp.int32
    )
    running = jnp.cumsum(onehot, axis=0) - onehot
    return jnp.sum(running * onehot, axis=1)


def soft_weights(scores, allowed):
    masked = jnp.where(allowed, scores, -1e30)
    largest = jnp.max(masked, axis=-1, keepdims=True)
    exponent = jnp.exp(masked - largest)
    return (exponent / jnp.sum(exponent, axis=-1, keepdims=True)).astype(jnp.bfloat16)


def per_device(
    hidden_in,
    segment_ids,
    attn_routes,
    ffn_routes,
    attn_gain,
    attn_router,
    w_query,
    w_key,
    w_value,
    w_out,
    ffn_gain,
    ffn_router,
    w_gate_up,
    w_down,
):
    row_count = hidden_in.shape[0]
    head_count = lax.axis_size("head")
    seq_length = row_count * head_count
    capacity = 3 * seq_length // 8
    local_width = w_key.shape[1]
    local_heads = local_width // HD
    normed = rms_norm(hidden_in, attn_gain)
    normed_all, segment_all, routes_all = (
        lax.all_gather(normed, "head", axis=0, tiled=True),
        lax.all_gather(segment_ids, "head", axis=1, tiled=True),
        lax.all_gather(attn_routes, "head", axis=0, tiled=True),
    )
    segment_row = segment_all[0]
    token_place = positions(segment_row)
    pair_weights = pair_gates(normed_all, attn_router, routes_all)
    flat_experts = routes_all.reshape(-1)
    slot_index = flat_experts * capacity + slot_ranks(flat_experts, E_ATT)
    slot_table = (
        jnp.full((E_ATT * capacity,), 2 * seq_length, jnp.int32)
        .at[slot_index]
        .set(jnp.arange(2 * seq_length, dtype=jnp.int32))
    )
    padded = jnp.concatenate([normed_all, jnp.zeros((1, D), jnp.bfloat16)], axis=0)
    buffer = padded[slot_table // 2].reshape(E_ATT, capacity, D)
    query_buf = jnp.einsum("ecd,edf->ecf", buffer, w_query, preferred_element_type=jnp.float32)
    queries = query_buf.reshape(E_ATT * capacity, local_width)[slot_index].reshape(
        seq_length, 2, local_heads, HD
    )
    queries = rotary(queries, token_place).astype(jnp.bfloat16)
    key_heads = jnp.dot(normed_all, w_key, preferred_element_type=jnp.float32).reshape(
        seq_length, local_heads, HD
    )
    key_heads = rotary(key_heads, token_place).astype(jnp.bfloat16)
    value_heads = (
        jnp.dot(normed_all, w_value, preferred_element_type=jnp.float32)
        .astype(jnp.bfloat16)
        .reshape(seq_length, local_heads, HD)
    )
    block_rows = min(seq_length, 512)
    block_total = seq_length // block_rows
    key_index = jnp.arange(seq_length, dtype=jnp.int32)

    def attend(block_input):
        query_block, offset = block_input
        scores = jnp.einsum(
            "tjgd,sgd->gjts", query_block, key_heads, preferred_element_type=jnp.float32
        ) * HD ** (-0.5)
        query_index = offset + jnp.arange(block_rows, dtype=jnp.int32)
        allowed = (segment_row[:, None] == segment_row[None, :]) & (
            key_index[None, :] <= query_index[:, None]
        )
        probs = soft_weights(scores, allowed)
        return jnp.einsum(
            "gjts,sgd->tjgd", probs, value_heads, preferred_element_type=jnp.float32
        ).astype(jnp.bfloat16)

    contexts = lax.map(
        attend,
        (
            queries.reshape(block_total, block_rows, 2, local_heads, HD),
            jnp.arange(block_total, dtype=jnp.int32) * block_rows,
        ),
    )
    context = contexts.reshape(2 * seq_length, local_width)
    padded_ctx = jnp.concatenate([context, jnp.zeros((1, local_width), jnp.bfloat16)], axis=0)
    out_buf = padded_ctx[slot_table].reshape(E_ATT, capacity, local_width)
    projected = jnp.einsum("ecf,efd->ecd", out_buf, w_out, preferred_element_type=jnp.float32)
    per_pair = (
        projected.reshape(E_ATT * capacity, D)[slot_index] * pair_weights.reshape(-1)[:, None]
    )
    partial_value = jnp.sum(per_pair.reshape(seq_length, 2, D), axis=1)
    attn_rows = lax.psum_scatter(
        partial_value.astype(jnp.bfloat16), "head", scatter_dimension=0, tiled=True
    ).astype(jnp.float32)
    residual = (hidden_in.astype(jnp.float32) + attn_rows).astype(jnp.bfloat16)
    ffn_normed = rms_norm(residual, ffn_gain)
    ffn_weights = pair_gates(ffn_normed, ffn_router, ffn_routes)
    cap_ffn = 3 * row_count // 8
    local_experts = w_gate_up.shape[0]
    experts_flat = ffn_routes.reshape(-1)
    destination = experts_flat * cap_ffn + slot_ranks(experts_flat, E_FF)
    send_table = (
        jnp.full((E_FF * cap_ffn,), 2 * row_count, jnp.int32)
        .at[destination]
        .set(jnp.arange(2 * row_count, dtype=jnp.int32))
    )
    padded_ffn = jnp.concatenate([ffn_normed, jnp.zeros((1, D), jnp.bfloat16)], axis=0)
    outgoing = padded_ffn[send_table // 2].reshape(head_count, local_experts * cap_ffn, D)
    arrived = lax.all_to_all(outgoing, "head", split_axis=0, concat_axis=0, tiled=True)
    shard_rows = lax.all_gather(arrived, "req", axis=0, tiled=True)
    row_total = shard_rows.shape[0]
    grouped = shard_rows.reshape(row_total, local_experts, cap_ffn, D)
    gate_up = jnp.einsum("mecd,edgf->mecgf", grouped, w_gate_up, preferred_element_type=jnp.float32)
    activated = (jax.nn.silu(gate_up[..., 0, :]) * gate_up[..., 1, :]).astype(jnp.bfloat16)
    partials = jnp.einsum(
        "mecf,efd->mecd", activated, w_down, preferred_element_type=jnp.float32
    ).astype(jnp.bfloat16)
    partials = lax.optimization_barrier(partials).astype(jnp.float32)
    summed = lax.psum_scatter(
        partials.reshape(lax.axis_size("req") * head_count, local_experts * cap_ffn, D).astype(
            jnp.bfloat16
        ),
        "req",
        scatter_dimension=0,
        tiled=True,
    )
    returned = lax.all_to_all(summed, "head", split_axis=0, concat_axis=0, tiled=True)
    expert_rows = returned.reshape(-1, D)[destination]
    mixture = jnp.sum(
        expert_rows.astype(jnp.float32).reshape(row_count, 2, D) * ffn_weights[:, :, None], axis=1
    )
    return (residual.astype(jnp.float32) + mixture).astype(jnp.bfloat16)


def solution(mesh):
    return jax.shard_map(
        per_device,
        mesh=mesh,
        in_specs=(
            P(("req", "head"), None),
            P("req", "head"),
            P(("req", "head"), None),
            P(("req", "head"), None),
            P(),
            P(),
            P(None, None, "head"),
            P(None, "head"),
            P(None, "head"),
            P(None, "head", None),
            P(),
            P(),
            P("head", None, None, "req"),
            P("head", "req", None),
        ),
        out_specs=P(("req", "head"), None),
        check_vma=False,
    )
```

profile of v0, /device:TPU:0, one launch (start us, length us, event | category | flops | bytes accessed | tf_op | source)
XLA Modules:
  0.0 355.4 jit_solution(13910258309612906082)
XLA Ops:
  6.5 1.2 fusion.22
  7.8 1.8 fusion.24
  9.7 12.8 %all-gather = s32[4,64,2]{1,2,0:T(2,128)S(1)} all-gather(s32[1,64,2]{1,2,0:T(2,128)} %bitcast.132), channel_id=1, replica_groups=mesh['req'=8,'head'=4] {'head'}, dimensions={0}, use_global_device_ids=true | all-gather | bytes 2560 | tf_op jit(solution)/shard_map/all_gather | solution.py:91
  23.0 1.2 reduce-window.6
  24.1 0.2 slice_reduce_fusion
  24.4 0.1 eq.66
  24.5 0.1 copy.116
  24.7 0.1 mul.215
  24.9 1.3 dynamic-slice.1
  26.9 0.8 bitcast_dynamic-update-slice_fusion
  27.8 0.1 reshape.375
  28.0 2.4 scatter_custom_fusion
  30.4 6.0 %all-reduce.3 = s32[256]{0:T(256)S(1)} all-reduce(s32[256]{0:T(256)S(1)} %bitcast_dynamic-update-slice_fusion), channel_id=1, replica_groups=mesh['req'=8,'head'=4] {'head'}, use_global_device_ids=true, to_apply=%add.3 | all-reduce | flops 256 | bytes 2048 | tf_op jit(solution)/shard_map/while/body/eval_jaxpr/eq | solution.py:129
  36.7 0.5 multiply_cosine_fusion
  37.3 3.3 all-gather.4.cloned.1.call-done
  40.6 1.3 concatenate.18
  41.9 4.8 %gather_fusion = bf16[768,2048]{1,0:T(8,128)(2,1)} fusion(bf16[257,2048]{1,0:T(8,128)(2,1)S(1)} %concatenate.18, s32[1024]{0:T(1024)S(1)} %pad_clamp_fusion.4), kind=kCustom, calls=%fused_computation | custom fusion | bytes 6294528 | tf_op jit(solution)/shard_map/gather | solution.py:104
  46.7 10.6 %fusion.66 = f32[8,96,512]{2,1,0:T(8,128)} fusion(bf16[8,96,2048]{2,1,0:T(8,128)(2,1)} %bitcast.122, bf16[8,2048,512]{2,1,0:T(8,128)(2,1)} %param.20), kind=kOutput, calls=%fused_computation.131 | convolution fusion | flops 1610612736 | bytes 21495808 | tf_op jit(solution)/shard_map/ecd,edf->ecf/dot_general | solution.py:105
  57.3 4.1 %gather_fusion.1 = f32[512,512]{1,0:T(8,128)} fusion(f32[768,512]{1,0:T(8,128)} %bitcast.119, s32[1024]{0:T(1024)S(1)} %pad_clamp_fusion.3), kind=kCustom, calls=%fused_computation.1 | custom fusion | bytes 2099200 | tf_op jit(solution)/shard_map/gather | solution.py:106
  61.5 1.6 reshape.317
  63.0 2.1 fusion.60
  65.1 1.5 fusion.65
  66.6 1.3 reshape.313
  67.9 1.1 fusion.61
  69.1 3.1 convolution_convert_fusion.1
  72.2 1.8 copy.142
  73.9 2.6 subtract_convert_fusion
  76.6 0.1 subtract_convert_fusion.1
  76.7 3.6 %fusion.62 = (f32[4,2,256]{2,1,0:T(2,128)S(1)}, f32[4,2,256,256]{2,3,1,0:T(8,128)}) fusion(pred[256,256]{0,1:T(8,128)(4,1)S(1)} %fusion.36, bf16[256,2,4,64]{3,0,1,2:T(8,128)(2,1)} %get-tuple-element.18, bf16[256,2,4,64]{3,0,1,2:T(8,128)(2,1)} %get-tuple-element.17, bf16[256,4,64]{2,0,1:T(8,128)(2,1)S(1)} %get-tuple-element.20, ...), kind=kOutput, calls=%fused_computation.129 | convolution fusion | flops 137888000 | bytes 2957312 | tf_op jit(solution)/shard_map/while/body/eval_jaxpr/sub | solution.py:61
  80.4 1.9 fusion.18
  82.3 0.3 copy.124
  82.7 2.7 gather_fusion.2
  85.4 11.2 %fusion.67 = f32[8,96,2048]{2,1,0:T(8,128)} fusion(bf16[8,96,512]{2,1,0:T(8,128)(2,1)S(1)} %bitcast.123, bf16[8,512,2048]{2,1,0:T(8,128)(2,1)} %param.23), kind=kOutput, calls=%fused_computation.132 | convolution fusion | flops 1610612736 | bytes 23855104 | tf_op jit(solution)/shard_map/ecf,efd->ecd/dot_general | solution.py:147
  96.6 8.4 %gather_fusion.3 = f32[512,2048]{1,0:T(8,128)} fusion(f32[768,2048]{1,0:T(8,128)} %bitcast.118, s32[1024]{0:T(1024)S(1)} %pad_clamp_fusion.3), kind=kCustom, calls=%fused_computation.3 | custom fusion | bytes 8390656 | tf_op jit(solution)/shard_map/gather | solution.py:149
  105.0 5.9 %gather.32 = f32[256,2,2048]{2,1,0:T(2,128)} reshape(f32[512,2048]{1,0:T(8,128)} %gather_fusion.3) | data formatting | bytes 8388608 | tf_op jit(solution)/shard_map/gather | solution.py:149
  110.9 0.9 fusion.68
  111.8 3.5 gather_fusion.6
  115.3 0.1 reshape.378
  115.6 0.1 copy.127
  115.8 9.9 %multiply_reduce_fusion = bf16[256,2048]{1,0:T(8,128)(2,1)} fusion(f32[256,2,2048]{2,1,0:T(2,128)} %gather.32, f32[256,2]{1,0:T(8,128)S(1)} %copy.127), kind=kLoop, calls=%fused_computation.21 | loop fusion | flops 1572864 | bytes 5244928 | tf_op jit(solution)/shard_map/reduce_sum | solution.py:151
  125.8 0.1 eq.74
  126.0 0.2 reduce_window_sum.28
  126.3 0.1 mul.234
  126.5 0.2 select_reduce_fusion
  126.7 1.2 scatter_custom_fusion.1
  127.9 24.6 %reduce-scatter.3.cloned.1.call-done = bf16[64,2048]{1,0:T(8,128)(2,1)} async-done(((bf16[256,2048]{1,0:T(8,128)(2,1)}), bf16[64,2048]{1,0:T(8,128)(2,1)}) %reduce-scatter.3.cloned.1.call-update) | async-done | bytes 262160 | tf_op jit(solution)/shard_map/reduce_scatter | solution.py:152
  152.5 1.1 fusion.26
  153.6 1.1 fusion.28
  154.7 1.1 gather_fusion.4
  155.9 23.3 %all_to_all.10 = bf16[4,48,2048]{2,1,0:T(8,128)(2,1)} all-to-all(bf16[4,48,2048]{2,1,0:T(8,128)(2,1)S(1)} %bitcast.124), channel_id=1, replica_groups=mesh['req'=8,'head'=4] {'head'}, dimensions={0} | all-to-all | bytes 1572864 | tf_op jit(solution)/shard_map/all_to_all | solution.py:169
  179.3 44.7 %all-gather.6.cloned.1.call-done = bf16[32,48,2048]{2,1,0:T(8,128)(2,1)} async-done(((bf16[4,48,2048]{2,1,0:T(8,128)(2,1)}), bf16[32,48,2048]{2,1,0:T(8,128)(2,1)}) %all-gather.6.cloned.1.call-update) | async-done | bytes 6291472 | tf_op jit(solution)/shard_map/all_gather | solution.py:170
  224.0 16.9 %fusion.10 = f32[32,2,24,2,704]{4,2,3,0,1:T(8,128)} fusion(bf16[2,2048,2,704]{1,3,2,0:T(8,128)(2,1)} %param.26, bf16[32,2,24,2048,1]{3,2,1,0,4:T(8,128)(2,1)} %bitcast.133), kind=kOutput, calls=%fused_computation.22 | convolution fusion | flops 8858370048 | bytes 26476544 | tf_op jit(solution)/shard_map/mecd,edgf->mecgf/dot_general | solution.py:173
  240.8 9.6 %convert_bitcast_fusion = bf16[32,2,24,2048]{3,2,0,1:T(8,128)(2,1)S(1)} fusion(bf16[2,704,2048]{2,1,0:T(8,128)(2,1)} %param.27, f32[32,2,24,2,704]{4,2,3,0,1:T(8,128)} %fusion.10), kind=kOutput, calls=%fused_computation.14 | convolution fusion | flops 4438818816 | bytes 20709376 | tf_op jit(solution)/shard_map/mecf,efd->mecd/dot_general | solution.py:175
  250.5 3.2 copy.132
  253.7 61.9 %reduce-scatter.5.cloned.1.call-done = bf16[4,48,2048]{2,1,0:T(8,128)(2,1)} async-done(((bf16[32,48,2048]{2,1,0:T(8,128)(2,1)}), bf16[4,48,2048]{2,1,0:T(8,128)(2,1)}) %reduce-scatter.5.cloned.1.call-update) | async-done | bytes 786448 | tf_op jit(solution)/shard_map/reduce_scatter | solution.py:179
  315.6 4.9 %all-to-all-start.1 = ((bf16[4,48,2048]{2,1,0:T(8,128)(2,1)}), bf16[4,48,2048]{2,1,0:T(8,128)(2,1)S(1)}, u32[]{:S(2)}, u32[]{:S(2)}) async-start(bf16[4,48,2048]{2,1,0:T(8,128)(2,1)} %reduce-scatter.5.cloned.1.call-done), calls=%async_computation.3 | async-start | bytes 1572864 | tf_op jit(solution)/shard_map/all_to_all | solution.py:187
  320.6 0.1 reshape.381
  320.7 0.3 fusion.69
  321.0 1.0 gather_fusion.7
  322.5 18.1 %all-to-all-done.1 = bf16[4,48,2048]{2,1,0:T(8,128)(2,1)S(1)} async-done(((bf16[4,48,2048]{2,1,0:T(8,128)(2,1)}), bf16[4,48,2048]{2,1,0:T(8,128)(2,1)S(1)}, u32[]{:S(2)}, u32[]{:S(2)}) %all-to-all-start.1) | async-done | bytes 786464 | tf_op jit(solution)/shard_map/all_to_all | solution.py:187
  340.6 1.7 gather_fusion.5
  342.3 2.7 reshape.326
  345.0 2.8 multiply_reduce_fusion.1
  347.8 0.8 fusion.29
  (83 shorter events, 2.2 us)
Async XLA Ops:
  6.5 58.6 %copy-start = (bf16[2048,512]{1,0:T(8,128)(2,1)S(1)}, bf16[2048,512]{1,0:T(8,128)(2,1)}, u32[]{:S(2)}) copy-start(bf16[2048,512]{1,0:T(8,128)(2,1)} %param.21) | copy-start | bytes 6291460
  6.5 34.0 %all-gather.4.cloned.1.call-start = ((), (), s32[]{:S(2)}) async-start(), calls=%async_computation.4 | async-start | bytes 1310720 | tf_op jit(solution)/shard_map/all_gather | solution.py:89
  9.6 142.9 %reduce-scatter.3.cloned.1.call-start = ((), (), s32[]{:S(2)}) async-start(), calls=%async_computation.5 | async-start | bytes 1310720 | tf_op jit(solution)/shard_map/reduce_scatter | solution.py:152
  63.0 2.1 copy-start.3
  65.1 4.0 %copy-start.4 = (bf16[256,2048]{1,0:T(8,128)(2,1)S(1)}, bf16[256,2048]{1,0:T(8,128)(2,1)}, u32[]{:S(2)}) copy-start(bf16[256,2048]{1,0:T(8,128)(2,1)} %all-gather.4.cloned.1.call-done) | copy-start | bytes 3145732
  66.6 7.3 %copy-start.5 = (f32[256,2,4,64]{3,2,1,0:T(4,128)S(1)}, f32[256,2,4,64]{3,2,1,0:T(4,128)}, u32[]{:S(2)}) copy-start(f32[256,2,4,64]{3,2,1,0:T(4,128)} %get-tuple-element.28) | copy-start | bytes 1572868
  69.1 7.5 %copy-start.7 = (f32[256,4,64]{2,1,0:T(4,128)S(1)}, f32[256,4,64]{2,1,0:T(4,128)}, u32[]{:S(2)}) copy-start(f32[256,4,64]{2,1,0:T(4,128)} %get-tuple-element.33) | copy-start | bytes 786436
  76.6 3.8 %copy-start.8 = (bf16[256,512]{0,1:T(8,128)(2,1)S(1)}, bf16[256,512]{0,1:T(8,128)(2,1)}, u32[]{:S(2)}) copy-start(bf16[256,512]{0,1:T(8,128)(2,1)} %copy.142) | copy-start | bytes 786436
  105.0 5.9 %copy-start.9 = (f32[2048,8]{0,1:T(8,128)S(1)}, f32[2048,8]{0,1:T(8,128)}, u32[]{:S(2)}) copy-start(f32[2048,8]{0,1:T(8,128)} %param.19) | copy-start | bytes 196612
  115.3 10.4 %copy-start.11 = (s32[64,2]{0,1:T(2,128)S(1)}, s32[64,2]{0,1:T(2,128)}, u32[]{:S(2)}) copy-start(s32[64,2]{0,1:T(2,128)} %param.17) | copy-start | bytes 1540
  115.3 37.2 %copy-start.2 = (bf16[64,2048]{1,0:T(8,128)(2,1)S(1)}, bf16[64,2048]{1,0:T(8,128)(2,1)}, u32[]{:S(2)}) copy-start(bf16[64,2048]{1,0:T(8,128)(2,1)} %param.14) | copy-start | bytes 786436
  115.3 38.3 %copy-start.12 = (f32[2048]{0:T(1024)S(1)}, f32[2048]{0:T(1024)}, u32[]{:S(2)}) copy-start(f32[2048]{0:T(1024)} %param.24) | copy-start | bytes 24580
  125.7 98.3 %all-gather.6.cloned.1.call-start = ((), (), s32[]{:S(2)}) async-start(), calls=%async_computation.6 | async-start | bytes 7077888 | tf_op jit(solution)/shard_map/all_gather | solution.py:170
  179.3 136.4 %reduce-scatter.5.cloned.1.call-start = ((), (), s32[]{:S(2)}) async-start(), calls=%async_computation.7 | async-start | bytes 7077888 | tf_op jit(solution)/shard_map/reduce_scatter | solution.py:179
  253.7 67.0 %copy-start.10 = (f32[2048,8]{0,1:T(8,128)S(1)}, f32[2048,8]{0,1:T(8,128)}, u32[]{:S(2)}) copy-start(f32[2048,8]{0,1:T(8,128)} %param.25) | copy-start | bytes 196612
  315.6 25.0 %all-to-all-start.1 = ((bf16[4,48,2048]{2,1,0:T(8,128)(2,1)}), bf16[4,48,2048]{2,1,0:T(8,128)(2,1)S(1)}, u32[]{:S(2)}, u32[]{:S(2)}) async-start(bf16[4,48,2048]{2,1,0:T(8,128)(2,1)} %reduce-scatter.5.cloned.1.call-done), calls=%async_computation.3 | async-start | bytes 1572864 | tf_op jit(solution)/shard_map/all_to_all | solution.py:187
  322.1 25.7 %copy-start.6 = (bf16[64,2048]{1,0:T(8,128)(2,1)S(1)}, bf16[64,2048]{1,0:T(8,128)(2,1)}, u32[]{:S(2)}) copy-start(bf16[64,2048]{1,0:T(8,128)(2,1)} %reduce-scatter.3.cloned.1.call-done) | copy-start | bytes 786436
  340.6 8.0 %copy-start.1 = (bf16[2048,512]{1,0:T(8,128)(2,1)S(1)}, bf16[2048,512]{1,0:T(8,128)(2,1)}, u32[]{:S(2)}) copy-start(bf16[2048,512]{1,0:T(8,128)(2,1)} %param.21) | copy-start | bytes 6291460
Sparse Core Ops, SparseCore 0:
  9.7 30.7 all-gather.3
  125.8 26.6 reduce-scatter.2
  179.4 44.5 all-gather.5
  253.8 61.7 reduce-scatter.4
where the time goes:
time: 359 us; the launch traced here: 355 us
  waiting for transfers between devices  153 us (43%)
  matrix products  59.7 us (17%)
  local copies, waits for them, and re-layouts  57.3 us (16%)
  blocking collectives  42.2 us (12%)
  other arithmetic  24.1 us (7%)
  between operations  14.6 us (4%)
  starting transfers between devices  4.98 us (1%)
    reduce_scatter x1, waiting for transfers between devices, per_device(): lax.psum_scatter(partials.reshape(lax.axis_size('req') * head_count, loca...  61.9 us
    all_gather x1, waiting for transfers between devices, per_device(): shard_rows = lax.all_gather(arrived, 'req', axis=0, tiled=True)  44.7 us
    reduce_scatter x1, waiting for transfers between devices, per_device(): lax.psum_scatter(partial_value.astype(jnp.bfloat16), 'head', scatter_dime...  24.6 us
    all_to_all x1, blocking collectives, per_device(): lax.all_to_all(outgoing, 'head', split_axis=0, concat_axis=0, tiled=True)  23.3 us
    all_to_all x1, waiting for transfers between devices, per_device(): lax.all_to_all(summed, 'head', split_axis=0, concat_axis=0, tiled=True)  18.1 us
    dot_general x1, matrix products, per_device(): jnp.einsum('mecd,edgf->mecgf', grouped, w_gate_up, preferred_element_type...  16.9 us
    gather x2, local copies, waits for them, and re-layouts, per_device(): projected.reshape(E_ATT * capacity, D)[slot_index]  14.3 us
    all_gather x1, blocking collectives, per_device(): lax.all_gather(attn_routes, 'head', axis=0, tiled=True)  12.8 us
  transfers between devices with their start and end apart: 5, of which 5 were waited for; matrix products, arithmetic and copies ran while one was open for 3% of the time, Pallas kernels for 0%

commit v1 on v0

v1 whole, which is shorter than its diff:
```python
import functools

import jax
import jax.numpy as jnp
from jax import lax
from jax.experimental import pallas as pl
from jax.experimental.pallas import tpu as pltpu
from jax.sharding import PartitionSpec as P

D = 2048
HD = 128
E_ATT = 8
E_FF = 8


EPSILON = 1e-06
ROPE_BASE = 10000.0


def rms_norm(values, gain_vector):
    widened = values.astype(jnp.float32)
    inverse_rms = lax.rsqrt(jnp.mean(widened * widened, axis=-1, keepdims=True) + EPSILON)
    return (widened * inverse_rms * gain_vector).astype(jnp.bfloat16)


def pair_gates(normed, router, routes):
    logits = jnp.dot(normed.astype(jnp.float32), router, precision=lax.Precision.HIGHEST)
    experts = jnp.arange(router.shape[1], dtype=jnp.int32)
    onehot = (routes[:, :, None] == experts).astype(jnp.float32)
    picked = jnp.sum(onehot * logits[:, None, :], axis=2)
    return jax.nn.sigmoid(picked - picked[:, ::-1])


def positions(segment_row):
    earlier = (segment_row[None, :] < segment_row[:, None]).astype(jnp.int32)
    return jnp.arange(segment_row.shape[0], dtype=jnp.int32) - jnp.sum(earlier, axis=1)


def rotary_table(token_place):
    half_width = HD // 2
    inverse = ROPE_BASE ** (-jnp.arange(half_width, dtype=jnp.float32) / half_width)
    angles = token_place.astype(jnp.float32)[:, None] * inverse
    cosine = jnp.cos(angles)
    sines = jnp.sin(angles)
    return jnp.concatenate([cosine, cosine, -sines, sines], axis=1)


def rotate(head, table):
    return head * table[:, :HD] + pltpu.roll(head, HD // 2, 1) * table[:, HD:]


def attention_kernel(
    capacity, rows_ref, info_ref, table_ref, w_key_ref, w_value_ref, w_query_ref, w_out_ref,
    out_ref, keys, values, total,
):
    expert = pl.program_id(0)
    seq = rows_ref.shape[0]
    heads = w_key_ref.shape[1] // HD
    rows = rows_ref[...]

    @pl.when(expert == 0)
    def _():
        raw_keys = jnp.dot(rows, w_key_ref[...], preferred_element_type=jnp.float32)
        for head in range(heads):
            part = raw_keys[:, head * HD : (head + 1) * HD]
            keys[:, head * HD : (head + 1) * HD] = rotate(part, table_ref[...]).astype(jnp.bfloat16)
        values[...] = jnp.dot(
            rows, w_value_ref[...], preferred_element_type=jnp.float32
        ).astype(jnp.bfloat16)
        total[...] = jnp.zeros_like(total)

    own = expert.astype(jnp.float32)
    first, second = info_ref[0:1, :] == own, info_ref[1:2, :] == own
    member = (first | second).astype(jnp.float32)
    gates = jnp.where(first, info_ref[2:3, :], jnp.where(second, info_ref[3:4, :], 0.0))
    segments = info_ref[4:5, :]
    earlier = (
        lax.broadcasted_iota(jnp.int32, (seq, seq), 0)
        < lax.broadcasted_iota(jnp.int32, (seq, seq), 1)
    ).astype(jnp.float32).astype(jnp.bfloat16)
    rank = jnp.dot(
        jnp.broadcast_to(member, (16, seq)).astype(jnp.bfloat16), earlier,
        preferred_element_type=jnp.float32,
    )[0:1, :]
    slots = lax.broadcasted_iota(jnp.int32, (capacity, seq), 0).astype(jnp.float32)
    place = lax.broadcasted_iota(jnp.int32, (capacity, seq), 1).astype(jnp.float32)
    pick = jnp.where((slots == rank) & (member > 0.0), 1.0, 0.0)
    pick_half = pick.astype(jnp.bfloat16)
    slot_gate = jnp.sum(pick * gates, axis=1, keepdims=True)
    slot_segment = jnp.sum(pick * segments, axis=1, keepdims=True)
    slot_place = jnp.sum(pick * place, axis=1, keepdims=True)
    slot_table = jnp.dot(
        pick, table_ref[...], precision=lax.Precision.HIGHEST, preferred_element_type=jnp.float32
    )
    allowed = (slot_segment == segments) & (place <= slot_place)
    picked = jnp.dot(pick_half, rows, preferred_element_type=jnp.float32).astype(jnp.bfloat16)
    raw = jnp.dot(picked, w_query_ref[0], preferred_element_type=jnp.float32)
    contexts = []
    for head in range(heads):
        span = slice(head * HD, (head + 1) * HD)
        query = rotate(raw[:, span], slot_table).astype(jnp.bfloat16)
        scores = lax.dot_general(
            query, keys[:, span], (((1,), (1,)), ((), ())), preferred_element_type=jnp.float32
        ) * HD ** (-0.5)
        masked = jnp.where(allowed, scores, -1e30)
        exponent = jnp.exp(masked - jnp.max(masked, axis=1, keepdims=True))
        probs = (exponent / jnp.sum(exponent, axis=1, keepdims=True)).astype(jnp.bfloat16)
        contexts.append(
            jnp.dot(probs, values[:, span], preferred_element_type=jnp.float32).astype(jnp.bfloat16)
        )
    context = jnp.concatenate(contexts, axis=1)
    projected = jnp.dot(context, w_out_ref[0], preferred_element_type=jnp.float32)
    weighted = (projected * slot_gate).astype(jnp.bfloat16)
    total[...] += lax.dot_general(
        pick_half, weighted, (((0,), (0,)), ((), ())), preferred_element_type=jnp.float32
    )

    @pl.when(expert == pl.num_programs(0) - 1)
    def _():
        out_ref[...] = total[...].astype(jnp.bfloat16)


def attention(rows, info, table, w_key, w_value, w_query, w_out, capacity):
    seq, width = rows.shape[0], w_key.shape[1]
    whole = lambda shape: pl.BlockSpec(shape, lambda e: (0,) * len(shape))
    return pl.pallas_call(
        functools.partial(attention_kernel, capacity),
        grid=(E_ATT,),
        out_shape=jax.ShapeDtypeStruct((seq, D), jnp.bfloat16),
        in_specs=[
            whole((seq, D)),
            whole(info.shape),
            whole(table.shape),
            whole((D, width)),
            whole((D, width)),
            pl.BlockSpec((1, D, width), lambda e: (e, 0, 0)),
            pl.BlockSpec((1, width, D), lambda e: (e, 0, 0)),
        ],
        out_specs=whole((seq, D)),
        scratch_shapes=[
            pltpu.VMEM((seq, width), jnp.bfloat16),
            pltpu.VMEM((seq, width), jnp.bfloat16),
            pltpu.VMEM((seq, D), jnp.float32),
        ],
        compiler_params=pltpu.CompilerParams(vmem_limit_bytes=48 * 1024 * 1024),
        cost_estimate=pl.CostEstimate(
            flops=12 * 10**9, bytes_accessed=40 * 10**6, transcendentals=10**6
        ),
    )(rows, info, table, w_key, w_value, w_query, w_out)


def per_device(
    hidden_in,
    segment_ids,
    attn_routes,
    ffn_routes,
    attn_gain,
    attn_router,
    w_query,
    w_key,
    w_value,
    w_out,
    ffn_gain,
    ffn_router,
    w_gate_up,
    w_down,
):
    row_count = hidden_in.shape[0]
    head_count = lax.axis_size("head")
    seq_length = row_count * head_count
    capacity = 3 * seq_length // 8
    normed = rms_norm(hidden_in, attn_gain)
    labels = jnp.concatenate(
        [attn_routes, segment_ids.reshape(row_count, 1), jnp.zeros((row_count, 125), jnp.int32)],
        axis=1,
    ).astype(jnp.bfloat16)
    gathered = lax.all_gather(
        jnp.concatenate([normed, labels], axis=1), "head", axis=0, tiled=True
    )
    normed_all = gathered[:, :D]
    labels_all = gathered[:, D : D + 3].astype(jnp.int32)
    routes_all, segment_row = labels_all[:, :2], labels_all[:, 2]
    table = rotary_table(positions(segment_row))
    pair_weights = pair_gates(normed_all, attn_router, routes_all)
    info = jnp.concatenate(
        [
            routes_all.astype(jnp.float32),
            pair_weights,
            segment_row[:, None].astype(jnp.float32),
            jnp.zeros((seq_length, 3), jnp.float32),
        ],
        axis=1,
    ).T
    partial_value = attention(
        normed_all, info, table, w_key, w_value, w_query, w_out, capacity
    )
    attn_rows = lax.psum_scatter(
        partial_value, "head", scatter_dimension=0, tiled=True
    ).astype(jnp.float32)
    residual = (hidden_in.astype(jnp.float32) + attn_rows).astype(jnp.bfloat16)
    ffn_normed = rms_norm(residual, ffn_gain)
    ffn_weights = pair_gates(ffn_normed, ffn_router, ffn_routes)
    cap_ffn = 3 * row_count // 8
    local_experts = w_gate_up.shape[0]
    slot_count = E_FF * cap_ffn
    experts = jnp.arange(E_FF, dtype=jnp.int32)
    member = jnp.sum((ffn_routes[:, :, None] == experts).astype(jnp.float32), axis=1)
    order = jnp.arange(row_count, dtype=jnp.int32)
    earlier = (order[None, :] < order[:, None]).astype(jnp.float32)
    rank = jnp.dot(earlier, member, preferred_element_type=jnp.float32).astype(jnp.int32)
    picks = jnp.sum(
        jnp.where(ffn_routes[:, :, None] == experts, rank[:, None, :], 0), axis=2
    )
    destination = ffn_routes * cap_ffn + picks
    slot_of = destination[:, :, None] == jnp.arange(slot_count, dtype=jnp.int32)
    chosen = jnp.any(slot_of, axis=1).astype(jnp.bfloat16)
    outgoing = jnp.einsum(
        "ts,td->sd", chosen, ffn_normed, preferred_element_type=jnp.float32
    ).astype(jnp.bfloat16).reshape(head_count, local_experts * cap_ffn, D)
    arrived = lax.all_to_all(outgoing, "head", split_axis=0, concat_axis=0, tiled=True)
    shard_rows = lax.all_gather(arrived, "req", axis=0, tiled=True)
    row_total = shard_rows.shape[0]
    grouped = shard_rows.reshape(row_total, local_experts, cap_ffn, D)
    gate_up = jnp.einsum("mecd,edgf->mecgf", grouped, w_gate_up, preferred_element_type=jnp.float32)
    activated = (jax.nn.silu(gate_up[..., 0, :]) * gate_up[..., 1, :]).astype(jnp.bfloat16)
    partials = jnp.einsum(
        "mecf,efd->mecd", activated, w_down, preferred_element_type=jnp.float32
    ).astype(jnp.bfloat16)
    summed = lax.psum_scatter(
        partials.reshape(lax.axis_size("req") * head_count, local_experts * cap_ffn, D),
        "req",
        scatter_dimension=0,
        tiled=True,
    )
    returned = lax.all_to_all(summed, "head", split_axis=0, concat_axis=0, tiled=True)
    mixing = jnp.sum(jnp.where(slot_of, ffn_weights[:, :, None], 0.0), axis=1)
    mixture = jnp.dot(
        mixing,
        returned.reshape(slot_count, D).astype(jnp.float32),
        precision=lax.Precision.HIGHEST,
    )
    return (residual.astype(jnp.float32) + mixture).astype(jnp.bfloat16)


def solution(mesh):
    return jax.shard_map(
        per_device,
        mesh=mesh,
        in_specs=(
            P(("req", "head"), None),
            P("req", "head"),
            P(("req", "head"), None),
            P(("req", "head"), None),
            P(),
            P(),
            P(None, None, "head"),
            P(None, "head"),
            P(None, "head"),
            P(None, "head", None),
            P(),
            P(),
            P("head", None, None, "req"),
            P("head", "req", None),
        ),
        out_specs=P(("req", "head"), None),
        check_vma=False,
    )
```

time: 359 us -> 294 us (0.82)
  local copies, waits for them, and re-layouts: 57.3 us -> 6.75 us
  waiting for transfers between devices: 153 us -> 185 us
  matrix products: 59.7 us -> 30.8 us
  Pallas kernels: 0 us -> 23.5 us
  blocking collectives: 42.2 us -> 23.3 us
  other arithmetic: 24.1 us -> 6.17 us
    gather x17 -> x0, local copies, waits for them, and re-layouts: 34.2 us -> none  [the longest x2 14.3 us: per_device(): projected.reshape(E_ATT * capacity, D)[slot_index]]
    all_gather x1, waiting for transfers between devices: 3.32 us -> 31.7 us  [per_device(): lax.all_gather(jnp.concatenate([normed, labels], axis=1), 'head', axis=0,...]
    dot_general x5 -> x3, matrix products: 28.3 us -> 1.81 us  [the longest x1 1.24 us: per_device(): jnp.dot(mixing, returned.reshape(slot_count, D).astype(jnp.float32), prec...]
    pallas_call x0 -> x1, Pallas kernels: none -> 23.5 us  [attention(): pl.pallas_call(functools.partial(attention_kernel, capacity), grid=(E_ATT...]
    all_gather x1 -> x0, blocking collectives: 12.8 us -> none  [per_device(): lax.all_gather(attn_routes, 'head', axis=0, tiled=True)]
    reduce_sum x4, other arithmetic: 12.9 us -> 0.2 us  [the longest x1 0.11 us: per_device(): mixing = jnp.sum(jnp.where(slot_of, ffn_weights[:, :, None], 0.0), axis=1)]
    eq x1 -> x0, blocking collectives: 5.99 us -> none  [attend(): segment_row[:, None] == segment_row[None, :]]
    reshape x3 -> x1, local copies, waits for them, and re-layouts: 4.64 us -> 0.11 us  [per_device(): segment_ids.reshape(row_count, 1)]
  transfers between devices with their start and end apart: 5 -> 5, of which waited for: 5 -> 5; matrix products, arithmetic and copies ran while one was open for 3% -> 0% of each run, Pallas kernels for 0% -> 0%
where the time goes in v1:
time: 294 us
  waiting for transfers between devices  185 us (63%)
  matrix products  30.8 us (10%)
  Pallas kernels  23.5 us (8%)
  blocking collectives  23.3 us (8%)
  between operations  13.3 us (5%)
  local copies, waits for them, and re-layouts  6.75 us (2%)
  other arithmetic  6.17 us (2%)
  starting transfers between devices  4.92 us (2%)
    reduce_scatter x1, waiting for transfers between devices, per_device(): lax.psum_scatter(partials.reshape(lax.axis_size('req') * head_count, loca...  61.9 us
    all_gather x1, waiting for transfers between devices, per_device(): shard_rows = lax.all_gather(arrived, 'req', axis=0, tiled=True)  44.5 us
    all_gather x1, waiting for transfers between devices, per_device(): lax.all_gather(jnp.concatenate([normed, labels], axis=1), 'head', axis=0,...  31.7 us
    reduce_scatter x1, waiting for transfers between devices, per_device(): lax.psum_scatter(partial_value, 'head', scatter_dimension=0, tiled=True)  26.7 us
    pallas_call x1, Pallas kernels, attention(): pl.pallas_call(functools.partial(attention_kernel, capacity), grid=(E_ATT...  23.5 us
    all_to_all x1, blocking collectives, per_device(): lax.all_to_all(outgoing, 'head', split_axis=0, concat_axis=0, tiled=True)  23.3 us
    all_to_all x1, waiting for transfers between devices, per_device(): lax.all_to_all(summed, 'head', split_axis=0, concat_axis=0, tiled=True)  19.9 us
    dot_general x1, matrix products, per_device(): jnp.einsum('mecd,edgf->mecgf', grouped, w_gate_up, preferred_element_type...  16.9 us
  transfers between devices with their start and end apart: 5, of which 5 were waited for; matrix products, arithmetic and copies ran while one was open for 0% of the time, Pallas kernels for 0%

profile of v1, /device:TPU:0, one launch (start us, length us, event | category | flops | bytes accessed | tf_op | source)
XLA Modules:
  0.0 293.6 jit_solution(8423055828898325133)
XLA Ops:
  6.5 0.0 copy-start
  6.5 0.0 copy-start.2
  6.5 0.0 all-gather.3.cloned.1.call-start
  6.5 1.3 fusion.17
  7.8 0.7 convert.9
  8.5 0.1 copy.63
  8.6 0.7 convert_bitcast_fusion.1
  9.3 0.1 copy.64
  9.4 1.1 fusion.19
  10.5 0.8 concatenate.12
  11.3 0.0 all-gather.3.cloned.1.call-update
  11.3 0.0 reduce-scatter.7.cloned.1.call-start
  11.4 0.1 pad.7.clone
  11.5 31.7 %all-gather.3.cloned.1.call-done = bf16[256,2176]{1,0:T(8,128)(2,1)} async-done(((bf16[64,2176]{1,0:T(8,128)(2,1)}), bf16[256,2176]{1,0:T(8,128)(2,1)}) %all-gather.3.cloned.1.call-update) | async-done | bytes 1114128 | tf_op jit(solution)/shard_map/all_gather | solution.py:177
  43.2 0.8 slice.25
  44.0 0.1 copy.79
  44.1 0.0 copy-done
  44.2 2.1 fusion.30
  46.3 0.1 rev.6
  46.4 0.2 convert_reduce_fusion
  46.6 0.5 multiply_cosine_fusion
  47.2 0.2 pad_maximum_fusion.table_ref
  47.4 0.1 maximum_bitcast_fusion.info_ref
  47.4 1.3 slice.24.rows_ref
  48.8 0.0 copy-done.2
  48.8 0.0 copy-start.3
  48.8 0.0 copy-start.5
  48.8 0.0 copy-start.6
  48.8 0.0 copy-start.4
  48.8 23.5 %shard_map.136 = bf16[256,2048]{1,0:T(8,128)(2,1)} custom-call(bf16[256,2048]{1,0:T(8,128)(2,1)S(1)} %slice.24.rows_ref, f32[8,256]{1,0:T(8,128)S(1)} %maximum_bitcast_fusion.info_ref, f32[256,256]{1,0:T(8,128)S(1)} %pad_maximum_fusion.table_ref, bf16[2048,512]{1,0:T(8,128)(2,1)S(1)} %copy-done.2, bf16[2048,512]{1,0:T(8,128)(2,1)} %w_value_ref.1, ...), custom_call_target="tpu_custom_call" | custom-call | flops 12000000000 | bytes 40000000 | tf_op jit(solution)/shard_map/pallas_call | solution.py:126
  72.3 0.0 reduce-scatter.7.cloned.1.call-update
  72.3 0.0 all-gather.5.cloned.1.call-start
  72.4 26.7 %reduce-scatter.7.cloned.1.call-done = bf16[64,2048]{1,0:T(8,128)(2,1)} async-done(((bf16[256,2048]{1,0:T(8,128)(2,1)}), bf16[64,2048]{1,0:T(8,128)(2,1)}) %reduce-scatter.7.cloned.1.call-update) | async-done | bytes 262160 | tf_op jit(solution)/shard_map/reduce_scatter | solution.py:197
  99.1 0.0 copy-done.3
  99.1 1.1 fusion.21
  100.2 0.0 copy-done.5
  100.2 0.0 copy-done.6
  100.3 0.4 fusion.26
  100.6 0.0 copy-done.4
  100.7 0.1 convolution_convert_fusion.1
  100.8 0.1 fusion.24
  100.9 0.4 convolution_convert_fusion
  101.4 23.3 %all_to_all.10 = bf16[4,48,2048]{2,1,0:T(8,128)(2,1)} all-to-all(bf16[4,48,2048]{2,1,0:T(8,128)(2,1)S(1)} %bitcast.52), channel_id=1, replica_groups=mesh['req'=8,'head'=4] {'head'}, dimensions={0} | all-to-all | bytes 1572864 | tf_op jit(solution)/shard_map/all_to_all | solution.py:220
  124.7 0.0 all-gather.5.cloned.1.call-update
  124.8 0.2 reduce-scatter.5.cloned.1.call-start
  125.0 44.5 %all-gather.5.cloned.1.call-done = bf16[32,48,2048]{2,1,0:T(8,128)(2,1)} async-done(((bf16[4,48,2048]{2,1,0:T(8,128)(2,1)}), bf16[32,48,2048]{2,1,0:T(8,128)(2,1)}) %all-gather.5.cloned.1.call-update) | async-done | bytes 6291472 | tf_op jit(solution)/shard_map/all_gather | solution.py:221
  169.5 16.9 %fusion.9 = f32[32,2,24,2,704]{4,2,3,0,1:T(8,128)} fusion(bf16[2,2048,2,704]{1,3,2,0:T(8,128)(2,1)} %param.26, bf16[32,2,24,2048,1]{3,2,1,0,4:T(8,128)(2,1)} %bitcast.54), kind=kOutput, calls=%fused_computation.10 | convolution fusion | flops 8858370048 | bytes 26476544 | tf_op jit(solution)/shard_map/mecd,edgf->mecgf/dot_general | solution.py:224
  186.3 9.6 %convert_bitcast_fusion = bf16[32,2,24,2048]{3,2,0,1:T(8,128)(2,1)S(1)} fusion(bf16[2,704,2048]{2,1,0:T(8,128)(2,1)} %param.27, f32[32,2,24,2,704]{4,2,3,0,1:T(8,128)} %fusion.9), kind=kOutput, calls=%fused_computation.3 | convolution fusion | flops 4438818816 | bytes 20709376 | tf_op jit(solution)/shard_map/mecf,efd->mecd/dot_general | solution.py:226
  196.0 0.0 copy-start.1
  196.0 3.2 %copy.71 = bf16[32,2,24,2048]{3,2,1,0:T(8,128)(2,1)} copy(bf16[32,2,24,2048]{3,2,0,1:T(8,128)(2,1)S(1)} %convert_bitcast_fusion) | data formatting | bytes 12582912 | tf_op jit(solution)/shard_map/convert_element_type | solution.py:228
  199.2 0.0 reduce-scatter.5.cloned.1.call-update
  199.2 61.9 %reduce-scatter.5.cloned.1.call-done = bf16[4,48,2048]{2,1,0:T(8,128)(2,1)} async-done(((bf16[32,48,2048]{2,1,0:T(8,128)(2,1)}), bf16[4,48,2048]{2,1,0:T(8,128)(2,1)}) %reduce-scatter.5.cloned.1.call-update) | async-done | bytes 786448 | tf_op jit(solution)/shard_map/reduce_scatter | solution.py:229
  261.1 4.6 %all-to-all-start.1 = ((bf16[4,48,2048]{2,1,0:T(8,128)(2,1)}), bf16[4,48,2048]{2,1,0:T(8,128)(2,1)S(1)}, u32[]{:S(2)}, u32[]{:S(2)}) async-start(bf16[4,48,2048]{2,1,0:T(8,128)(2,1)} %reduce-scatter.5.cloned.1.call-done), calls=%async_computation.2 | async-start | bytes 1572864 | tf_op jit(solution)/shard_map/all_to_all | solution.py:235
  265.8 0.1 select_reduce_fusion
  265.9 19.9 %all-to-all-done.1 = bf16[4,48,2048]{2,1,0:T(8,128)(2,1)S(1)} async-done(((bf16[4,48,2048]{2,1,0:T(8,128)(2,1)}), bf16[4,48,2048]{2,1,0:T(8,128)(2,1)S(1)}, u32[]{:S(2)}, u32[]{:S(2)}) %all-to-all-start.1) | async-done | bytes 786464 | tf_op jit(solution)/shard_map/all_to_all | solution.py:235
  285.9 1.2 fusion.16
  287.1 0.0 copy-done.1
  (16 shorter events, 0.2 us)
Async XLA Ops:
  6.5 37.6 %copy-start = (f32[2048,8]{0,1:T(8,128)S(1)}, f32[2048,8]{0,1:T(8,128)}, u32[]{:S(2)}) copy-start(f32[2048,8]{0,1:T(8,128)} %param.19) | copy-start | bytes 196612
  6.5 42.2 %copy-start.2 = (bf16[2048,512]{1,0:T(8,128)(2,1)S(1)}, bf16[2048,512]{1,0:T(8,128)(2,1)}, u32[]{:S(2)}) copy-start(bf16[2048,512]{1,0:T(8,128)(2,1)} %w_key_ref.1) | copy-start | bytes 6291460
  6.5 36.6 %all-gather.3.cloned.1.call-start = ((), (), s32[]{:S(2)}) async-start(), calls=%async_computation.4 | async-start | bytes 1392640 | tf_op jit(solution)/shard_map/all_gather | solution.py:177
  11.3 87.8 %reduce-scatter.7.cloned.1.call-start = ((), (), s32[]{:S(2)}) async-start(), calls=%async_computation.7 | async-start | bytes 1310720 | tf_op jit(solution)/shard_map/reduce_scatter | solution.py:197
  48.8 50.3 %copy-start.3 = (bf16[64,2048]{1,0:T(8,128)(2,1)S(1)}, bf16[64,2048]{1,0:T(8,128)(2,1)}, u32[]{:S(2)}) copy-start(bf16[64,2048]{1,0:T(8,128)(2,1)} %param.14) | copy-start | bytes 786436
  48.8 51.5 %copy-start.5 = (f32[2048]{0:T(1024)S(1)}, f32[2048]{0:T(1024)}, u32[]{:S(2)}) copy-start(f32[2048]{0:T(1024)} %param.24) | copy-start | bytes 24580
  48.8 51.5 %copy-start.6 = (f32[2048,8]{0,1:T(8,128)S(1)}, f32[2048,8]{0,1:T(8,128)}, u32[]{:S(2)}) copy-start(f32[2048,8]{0,1:T(8,128)} %param.25) | copy-start | bytes 196612
  48.8 51.8 %copy-start.4 = (s32[64,2]{0,1:T(2,128)S(1)}, s32[64,2]{0,1:T(2,128)}, u32[]{:S(2)}) copy-start(s32[64,2]{0,1:T(2,128)} %param.17) | copy-start | bytes 1540
  72.3 97.2 %all-gather.5.cloned.1.call-start = ((), (), s32[]{:S(2)}) async-start(), calls=%async_computation.5 | async-start | bytes 7077888 | tf_op jit(solution)/shard_map/all_gather | solution.py:221
  124.8 136.4 %reduce-scatter.5.cloned.1.call-start = ((), (), s32[]{:S(2)}) async-start(), calls=%async_computation.6 | async-start | bytes 7077888 | tf_op jit(solution)/shard_map/reduce_scatter | solution.py:229
  196.0 91.2 %copy-start.1 = (f32[2048,8]{0,1:T(8,128)S(1)}, f32[2048,8]{0,1:T(8,128)}, u32[]{:S(2)}) copy-start(f32[2048,8]{0,1:T(8,128)} %param.19) | copy-start | bytes 196612
  261.1 24.7 %all-to-all-start.1 = ((bf16[4,48,2048]{2,1,0:T(8,128)(2,1)}), bf16[4,48,2048]{2,1,0:T(8,128)(2,1)S(1)}, u32[]{:S(2)}, u32[]{:S(2)}) async-start(bf16[4,48,2048]{2,1,0:T(8,128)(2,1)} %reduce-scatter.5.cloned.1.call-done), calls=%async_computation.2 | async-start | bytes 1572864 | tf_op jit(solution)/shard_map/all_to_all | solution.py:235
Sparse Core Ops, SparseCore 0:
  11.4 31.6 all-gather.2
  72.4 26.5 reduce-scatter.6
  124.9 44.5 all-gather.4
  199.4 61.7 reduce-scatter.4

commit v2 on v1

--- a/solution.py
+++ b/solution.py
@@ -149,6 +149,28 @@
     )(rows, info, table, w_key, w_value, w_query, w_out)
 
 
+def exchange(values, step):
+    pairs = [(i, i ^ step) for i in range(lax.axis_size("req"))]
+    return lax.ppermute(values, "req", pairs)
+
+
+def spread(block, order):
+    stack = block[None]
+    for step in order:
+        stack = jnp.concatenate([stack, exchange(stack, step)], axis=0)
+    return stack
+
+
+def collect(stack, order):
+    for step in order[::-1]:
+        kept = stack.shape[0] // 2
+        arrived = exchange(stack[kept:], step)
+        stack = (stack[:kept].astype(jnp.float32) + arrived.astype(jnp.float32)).astype(
+            jnp.bfloat16
+        )
+    return stack[0]
+
+
 def per_device(
     hidden_in,
     segment_ids,
@@ -216,23 +238,38 @@
     chosen = jnp.any(slot_of, axis=1).astype(jnp.bfloat16)
     outgoing = jnp.einsum(
         "ts,td->sd", chosen, ffn_normed, preferred_element_type=jnp.float32
-    ).astype(jnp.bfloat16).reshape(head_count, local_experts * cap_ffn, D)
-    arrived = lax.all_to_all(outgoing, "head", split_axis=0, concat_axis=0, tiled=True)
-    shard_rows = lax.all_gather(arrived, "req", axis=0, tiled=True)
-    row_total = shard_rows.shape[0]
-    grouped = shard_rows.reshape(row_total, local_experts, cap_ffn, D)
-    gate_up = jnp.einsum("mecd,edgf->mecgf", grouped, w_gate_up, preferred_element_type=jnp.float32)
-    activated = (jax.nn.silu(gate_up[..., 0, :]) * gate_up[..., 1, :]).astype(jnp.bfloat16)
-    partials = jnp.einsum(
-        "mecf,efd->mecd", activated, w_down, preferred_element_type=jnp.float32
-    ).astype(jnp.bfloat16)
-    summed = lax.psum_scatter(
-        partials.reshape(lax.axis_size("req") * head_count, local_experts * cap_ffn, D),
-        "req",
-        scatter_dimension=0,
-        tiled=True,
-    )
-    returned = lax.all_to_all(summed, "head", split_axis=0, concat_axis=0, tiled=True)
+    ).astype(jnp.bfloat16).reshape(head_count, local_experts, cap_ffn, D)
+    req_count = lax.axis_size("req")
+    steps = [1 << bit for bit in range(1, req_count.bit_length() - 1)]
+    orders = [steps + [1], steps[::-1] + [1]]
+    half_rows = head_count * cap_ffn // 2
+    results = []
+    for expert in range(local_experts):
+        arrived = lax.all_to_all(
+            outgoing[:, expert], "head", split_axis=0, concat_axis=0, tiled=True
+        ).reshape(2, half_rows, D)
+        stacks = [spread(arrived[half], orders[half]) for half in range(2)]
+        rows = jnp.concatenate(stacks, axis=0).reshape(-1, D)
+        gate_up = jnp.einsum(
+            "md,dgf->mgf", rows, w_gate_up[expert], preferred_element_type=jnp.float32
+        )
+        activated = (jax.nn.silu(gate_up[:, 0]) * gate_up[:, 1]).astype(jnp.bfloat16)
+        partials = (
+            jnp.dot(activated, w_down[expert], preferred_element_type=jnp.float32)
+            .astype(jnp.bfloat16)
+            .reshape(2, req_count, half_rows, D)
+        )
+        summed = jnp.stack([collect(partials[half], orders[half]) for half in range(2)])
+        results.append(
+            lax.all_to_all(
+                summed.reshape(head_count, cap_ffn, D),
+                "head",
+                split_axis=0,
+                concat_axis=0,
+                tiled=True,
+            )
+        )
+    returned = jnp.stack(results, axis=1)
     mixing = jnp.sum(jnp.where(slot_of, ffn_weights[:, :, None], 0.0), axis=1)
     mixture = jnp.dot(
         mixing,

time: 294 us -> 245 us (0.83)
  waiting for transfers between devices: 185 us -> 113 us
  starting transfers between devices: 4.92 us -> 32.8 us
  blocking collectives: 23.3 us -> 14.2 us
  other arithmetic: 6.17 us -> 9.95 us
    reduce_scatter x1 -> x0, waiting for transfers between devices: 61.9 us -> none  [per_device(): lax.psum_scatter(partials.reshape(lax.axis_size('req') * head_count, loca...]
    all_gather x1 -> x0, waiting for transfers between devices: 44.5 us -> none  [per_device(): shard_rows = lax.all_gather(arrived, 'req', axis=0, tiled=True)]
    ppermute x0 -> x24, waiting for transfers between devices: none -> 29.3 us  [exchange(): return lax.ppermute(values, 'req', pairs)]
    ppermute x0 -> x24, starting transfers between devices: none -> 21.9 us  [exchange(): return lax.ppermute(values, 'req', pairs)]
    all_to_all x1, blocking collectives: 23.3 us -> 14.2 us  [per_device(): lax.all_to_all(outgoing[:, expert], 'head', split_axis=0, concat_axis=0,...]
    all_to_all x1 -> x3, starting transfers between devices: 4.61 us -> 10.9 us  [the longest x2 7.22 us: per_device(): lax.all_to_all(summed.reshape(head_count, cap_ffn, D), 'head', split_axis...]
    all_to_all x1 -> x3, waiting for transfers between devices: 19.9 us -> 25.4 us  [the longest x2 18.1 us: per_device(): lax.all_to_all(summed.reshape(head_count, cap_ffn, D), 'head', split_axis...]
    convert_element_type x1 -> x0, local copies, waits for them, and re-layouts: 3.24 us -> none  [per_device(): partials = jnp.einsum('mecf,efd->mecd', activated, w_down, preferred_elem...]
  transfers between devices with their start and end apart: 5 -> 29, of which waited for: 5 -> 12; matrix products, arithmetic and copies ran while one was open for 0% -> 13% of each run, Pallas kernels for 0% -> 0%
where the time goes in v2:
time: 245 us; the launch traced here: 244 us
  waiting for transfers between devices  113 us (46%)
  starting transfers between devices  32.8 us (13%)
  matrix products  31.2 us (13%)
  Pallas kernels  23.5 us (10%)
  blocking collectives  14.2 us (6%)
  between operations  14.1 us (6%)
  other arithmetic  9.95 us (4%)
  local copies, waits for them, and re-layouts  5.1 us (2%)
    all_gather x1, waiting for transfers between devices, per_device(): lax.all_gather(jnp.concatenate([normed, labels], axis=1), 'head', axis=0,...  31.7 us
    ppermute x24, waiting for transfers between devices, exchange(): return lax.ppermute(values, 'req', pairs)  29.3 us
    reduce_scatter x1, waiting for transfers between devices, per_device(): lax.psum_scatter(partial_value, 'head', scatter_dimension=0, tiled=True)  26.8 us
    pallas_call x1, Pallas kernels, attention(): pl.pallas_call(functools.partial(attention_kernel, capacity), grid=(E_ATT...  23.5 us
    ppermute x24, starting transfers between devices, exchange(): return lax.ppermute(values, 'req', pairs)  21.9 us
    all_to_all x2, waiting for transfers between devices, per_device(): lax.all_to_all(summed.reshape(head_count, cap_ffn, D), 'head', split_axis...  18.1 us
    dot_general x2, matrix products, per_device(): jnp.einsum('md,dgf->mgf', rows, w_gate_up[expert], preferred_element_type...  15.9 us
    all_to_all x1, blocking collectives, per_device(): lax.all_to_all(outgoing[:, expert], 'head', split_axis=0, concat_axis=0,...  14.2 us
  transfers between devices with their start and end apart: 29, of which 12 were waited for; matrix products, arithmetic and copies ran while one was open for 13% of the time, Pallas kernels for 0%

profile of v2, /device:TPU:0, one launch (start us, length us, event | category | flops | bytes accessed | tf_op | source)
XLA Modules:
  0.0 244.0 jit_solution(7323415102809114038)
XLA Ops:
  6.5 1.3 fusion.21
  7.8 0.7 convert.13
  8.6 0.7 convert_bitcast_fusion
  9.4 1.1 fusion.23
  10.5 0.8 concatenate.48
  11.5 31.7 %all-gather.2.cloned.1.call-done = bf16[256,2176]{1,0:T(8,128)(2,1)} async-done(((bf16[64,2176]{1,0:T(8,128)(2,1)}), bf16[256,2176]{1,0:T(8,128)(2,1)}) %all-gather.2.cloned.1.call-update) | async-done | bytes 1114128 | tf_op jit(solution)/shard_map/all_gather | solution.py:199
  43.2 0.9 slice.221
  44.2 2.1 fusion.35
  46.5 0.2 convert_reduce_fusion
  46.7 0.5 multiply_cosine_fusion
  47.3 0.2 pad_maximum_fusion.11.table_ref
  47.7 23.5 %shard_map.136 = bf16[256,2048]{1,0:T(8,128)(2,1)} custom-call(bf16[256,2048]{1,0:T(8,128)(2,1)S(1)} %slice.220.rows_ref, f32[8,256]{1,0:T(8,128)S(1)} %maximum_bitcast_fusion.info_ref, f32[256,256]{1,0:T(8,128)S(1)} %pad_maximum_fusion.11.table_ref, bf16[2048,512]{1,0:T(8,128)(2,1)S(1)} %copy-done.2, bf16[2048,512]{1,0:T(8,128)(2,1)} %w_value_ref.1, ...), custom_call_target="tpu_custom_call" | custom-call | flops 12000000000 | bytes 40000000 | tf_op jit(solution)/shard_map/pallas_call | solution.py:126
  71.2 26.8 %reduce-scatter.4.cloned.1.call-done = bf16[64,2048]{1,0:T(8,128)(2,1)} async-done(((bf16[256,2048]{1,0:T(8,128)(2,1)}), bf16[64,2048]{1,0:T(8,128)(2,1)}) %reduce-scatter.4.cloned.1.call-update) | async-done | bytes 262160 | tf_op jit(solution)/shard_map/reduce_scatter | solution.py:219
  98.0 1.1 fusion.25
  99.2 0.4 fusion.30
  99.8 0.4 convolution_convert_fusion.2
  100.3 0.8 slice_bitcast_fusion.1
  101.1 14.2 %all_to_all.20 = bf16[4,24,2048]{2,1,0:T(8,128)(2,1)S(1)} all-to-all(bf16[4,24,2048]{2,1,0:T(8,128)(2,1)S(1)} %get-tuple-element.18), channel_id=1, replica_groups=mesh['req'=8,'head'=4] {'head'}, dimensions={0} | all-to-all | bytes 786432 | tf_op jit(solution)/shard_map/all_to_all | solution.py:248
  115.3 3.6 %all-to-all-start = ((bf16[4,24,2048]{2,1,0:T(8,128)(2,1)}), bf16[4,24,2048]{2,1,0:T(8,128)(2,1)S(1)}, u32[]{:S(2)}, u32[]{:S(2)}) async-start(bf16[4,24,2048]{2,1,0:T(8,128)(2,1)} %get-tuple-element.17), calls=%async_computation | async-start | bytes 786432 | tf_op jit(solution)/shard_map/all_to_all | solution.py:248
  119.0 1.5 collective-permute-start.12
  120.5 1.5 collective-permute-start.15
  122.0 0.7 constant_dynamic-update-slice_fusion.15
  122.7 7.3 %all-to-all-done = bf16[4,24,2048]{2,1,0:T(8,128)(2,1)S(1)} async-done(((bf16[4,24,2048]{2,1,0:T(8,128)(2,1)}), bf16[4,24,2048]{2,1,0:T(8,128)(2,1)S(1)}, u32[]{:S(2)}, u32[]{:S(2)}) %all-to-all-start) | async-done | bytes 393248 | tf_op jit(solution)/shard_map/all_to_all | solution.py:248
  130.0 1.5 collective-permute-start
  131.5 1.5 collective-permute-start.3
  133.0 0.6 collective-permute-start.13
  133.7 0.6 collective-permute-start.16
  134.3 3.4 %collective-permute-done = bf16[1,48,2048]{2,1,0:T(8,128)(2,1)S(1)} collective-permute-done((bf16[1,48,2048]{2,1,0:T(8,128)(2,1)S(1)}, bf16[1,48,2048]{2,1,0:T(8,128)(2,1)S(1)}, u32[]{:S(2)}, u32[]{:S(2)}) %collective-permute-start) | collective-permute-done | bytes 196640 | tf_op jit(solution)/shard_map/ppermute | solution.py:154
  137.8 1.5 collective-permute-start.1
  139.4 1.6 collective-permute-start.4
  141.1 6.7 %collective-permute-done.13 = bf16[2,48,2048]{2,1,0:T(8,128)(2,1)S(1)} collective-permute-done((bf16[2,48,2048]{2,1,0:T(8,128)(2,1)S(1)}, bf16[2,48,2048]{2,1,0:T(8,128)(2,1)S(1)}, u32[]{:S(2)}, u32[]{:S(2)}) %collective-permute-start.13) | collective-permute-done | bytes 393248 | tf_op jit(solution)/shard_map/ppermute | solution.py:154
  148.0 0.5 collective-permute-start.17
  148.6 4.0 %collective-permute-done.1 = bf16[2,48,2048]{2,1,0:T(8,128)(2,1)S(1)} collective-permute-done((bf16[2,48,2048]{2,1,0:T(8,128)(2,1)S(1)}, bf16[2,48,2048]{2,1,0:T(8,128)(2,1)S(1)}, u32[]{:S(2)}, u32[]{:S(2)}) %collective-permute-start.1) | collective-permute-done | bytes 393248 | tf_op jit(solution)/shard_map/ppermute | solution.py:154
  152.8 0.5 collective-permute-start.5
  153.8 9.5 %fusion = f32[768,2,704]{0,2,1:T(8,128)} fusion(bf16[768,2048,1]{1,0,2:T(8,128)(2,1)S(1)} %bitcast.100, bf16[2,2048,2,704]{1,3,2,0:T(8,128)(2,1)} %param.26), kind=kOutput, calls=%fused_computation | convolution fusion | flops 4429185024 | bytes 13238272 | tf_op jit(solution)/shard_map/md,dgf->mgf/dot_general | solution.py:253
  163.3 5.5 %convolution_convert_fusion = bf16[768,2048]{1,0:T(8,128)(2,1)S(1)} fusion(bf16[2,704,2048]{2,1,0:T(8,128)(2,1)S(1)} %bitcast.106, f32[768,2,704]{0,2,1:T(8,128)} %fusion), kind=kOutput, calls=%fused_computation.6 | convolution fusion | flops 2219409408 | bytes 10354688 | tf_op jit(solution)/shard_map/dot_general | solution.py:258
  168.8 0.2 fusion.39
  169.1 0.5 collective-permute-start.18
  169.9 6.3 %fusion.2 = f32[768,2,704]{0,2,1:T(8,128)} fusion(bf16[768,2048,1]{1,0,2:T(8,128)(2,1)S(1)} %bitcast.101, bf16[2,2048,2,704]{1,3,2,0:T(8,128)(2,1)S(1)} %bitcast.104), kind=kOutput, calls=%fused_computation.2 | convolution fusion | flops 4429185024 | bytes 13238272 | tf_op jit(solution)/shard_map/md,dgf->mgf/dot_general | solution.py:253
  176.2 5.5 %convolution_convert_fusion.1 = bf16[768,2048]{1,0:T(8,128)(2,1)S(1)} fusion(bf16[2,704,2048]{2,1,0:T(8,128)(2,1)S(1)} %bitcast.106, f32[768,2,704]{0,2,1:T(8,128)} %fusion.2), kind=kOutput, calls=%fused_computation.7 | convolution fusion | flops 2219409408 | bytes 10354688 | tf_op jit(solution)/shard_map/dot_general | solution.py:258
  181.7 0.2 fusion.38
  182.1 0.4 collective-permute-start.6
  182.5 0.3 fusion.13
  182.9 0.6 collective-permute-start.22
  183.5 0.3 fusion.14
  183.8 1.5 collective-permute-start.19
  185.3 0.3 fusion.15
  185.6 1.5 collective-permute-start.10
  187.1 0.3 fusion.16
  187.5 0.7 collective-permute-start.7
  188.1 6.8 %collective-permute-done.22 = bf16[2,48,2048]{2,1,0:T(8,128)(2,1)S(1)} collective-permute-done((bf16[2,48,2048]{2,1,0:T(8,128)(2,1)S(1)}, bf16[2,48,2048]{2,1,0:T(8,128)(2,1)S(1)}, u32[]{:S(2)}, u32[]{:S(2)}) %collective-permute-start.22) | collective-permute-done | bytes 393248 | tf_op jit(solution)/shard_map/ppermute | solution.py:154
  195.0 1.5 collective-permute-start.23
  196.7 0.9 collective-permute-start.20
  197.5 5.8 %collective-permute-done.10 = bf16[2,48,2048]{2,1,0:T(8,128)(2,1)S(1)} collective-permute-done((bf16[2,48,2048]{2,1,0:T(8,128)(2,1)S(1)}, bf16[2,48,2048]{2,1,0:T(8,128)(2,1)S(1)}, u32[]{:S(2)}, u32[]{:S(2)}) %collective-permute-start.10) | collective-permute-done | bytes 393248 | tf_op jit(solution)/shard_map/ppermute | solution.py:154
  203.4 1.5 collective-permute-start.11
  205.1 0.9 collective-permute-start.8
  206.0 2.6 %collective-permute-done.23 = bf16[1,48,2048]{2,1,0:T(8,128)(2,1)S(1)} collective-permute-done((bf16[1,48,2048]{2,1,0:T(8,128)(2,1)S(1)}, bf16[1,48,2048]{2,1,0:T(8,128)(2,1)S(1)}, u32[]{:S(2)}, u32[]{:S(2)}) %collective-permute-start.23) | collective-permute-done | bytes 196640 | tf_op jit(solution)/shard_map/ppermute | solution.py:154
  208.6 0.8 pad_maximum_fusion.10
  209.4 3.8 %all-to-all-start.3 = ((bf16[4,24,2048]{2,1,0:T(8,128)(2,1)}), bf16[4,24,2048]{2,1,0:T(8,128)(2,1)S(1)}, u32[]{:S(2)}, u32[]{:S(2)}) async-start(bf16[4,24,2048]{2,1,0:T(8,128)(2,1)} %bitcast.30), calls=%async_computation.3 | async-start | bytes 786432 | tf_op jit(solution)/shard_map/all_to_all | solution.py:264
  213.3 0.8 pad_maximum_fusion.7
  214.1 8.7 %all-to-all-done.3 = bf16[4,24,2048]{2,1,0:T(8,128)(2,1)S(1)} async-done(((bf16[4,24,2048]{2,1,0:T(8,128)(2,1)}), bf16[4,24,2048]{2,1,0:T(8,128)(2,1)S(1)}, u32[]{:S(2)}, u32[]{:S(2)}) %all-to-all-start.3) | async-done | bytes 393248 | tf_op jit(solution)/shard_map/all_to_all | solution.py:264
  222.8 3.5 %all-to-all-start.1 = ((bf16[4,24,2048]{2,1,0:T(8,128)(2,1)}), bf16[4,24,2048]{2,1,0:T(8,128)(2,1)S(1)}, u32[]{:S(2)}, u32[]{:S(2)}) async-start(bf16[4,24,2048]{2,1,0:T(8,128)(2,1)} %bitcast.16), calls=%async_computation.1 | async-start | bytes 786432 | tf_op jit(solution)/shard_map/all_to_all | solution.py:264
  226.5 9.4 %all-to-all-done.1 = bf16[4,24,2048]{2,1,0:T(8,128)(2,1)S(1)} async-done(((bf16[4,24,2048]{2,1,0:T(8,128)(2,1)}), bf16[4,24,2048]{2,1,0:T(8,128)(2,1)S(1)}, u32[]{:S(2)}, u32[]{:S(2)}) %all-to-all-start.1) | async-done | bytes 393248 | tf_op jit(solution)/shard_map/all_to_all | solution.py:264
  235.9 1.2 fusion.10
  (124 shorter events, 3.7 us)
Async XLA Ops:
  6.5 37.7 %copy-start = (f32[2048,8]{0,1:T(8,128)S(1)}, f32[2048,8]{0,1:T(8,128)}, u32[]{:S(2)}) copy-start(f32[2048,8]{0,1:T(8,128)} %param.19) | copy-start | bytes 196612
  6.5 41.1 %copy-start.2 = (bf16[2048,512]{1,0:T(8,128)(2,1)S(1)}, bf16[2048,512]{1,0:T(8,128)(2,1)}, u32[]{:S(2)}) copy-start(bf16[2048,512]{1,0:T(8,128)(2,1)} %w_key_ref.1) | copy-start | bytes 6291460
  6.5 36.6 %all-gather.2.cloned.1.call-start = ((), (), s32[]{:S(2)}) async-start(), calls=%async_computation.5 | async-start | bytes 1392640 | tf_op jit(solution)/shard_map/all_gather | solution.py:199
  11.3 86.7 %reduce-scatter.4.cloned.1.call-start = ((), (), s32[]{:S(2)}) async-start(), calls=%async_computation.6 | async-start | bytes 1310720 | tf_op jit(solution)/shard_map/reduce_scatter | solution.py:219
  43.2 4.4 %copy-start.3 = (bf16[256,2176]{1,0:T(8,128)(2,1)S(1)}, bf16[256,2176]{1,0:T(8,128)(2,1)}, u32[]{:S(2)}) copy-start(bf16[256,2176]{1,0:T(8,128)(2,1)} %all-gather.2.cloned.1.call-done) | copy-start | bytes 3342340
  47.7 50.3 %copy-start.4 = (bf16[64,2048]{1,0:T(8,128)(2,1)S(1)}, bf16[64,2048]{1,0:T(8,128)(2,1)}, u32[]{:S(2)}) copy-start(bf16[64,2048]{1,0:T(8,128)(2,1)} %param.14) | copy-start | bytes 786436
  47.7 51.5 %copy-start.7 = (f32[2048]{0:T(1024)S(1)}, f32[2048]{0:T(1024)}, u32[]{:S(2)}) copy-start(f32[2048]{0:T(1024)} %param.24) | copy-start | bytes 24580
  47.7 51.5 %copy-start.8 = (f32[2048,8]{0,1:T(8,128)S(1)}, f32[2048,8]{0,1:T(8,128)}, u32[]{:S(2)}) copy-start(f32[2048,8]{0,1:T(8,128)} %param.25) | copy-start | bytes 196612
  47.7 51.8 %copy-start.6 = (s32[64,2]{0,1:T(2,128)S(1)}, s32[64,2]{0,1:T(2,128)}, u32[]{:S(2)}) copy-start(s32[64,2]{0,1:T(2,128)} %param.17) | copy-start | bytes 1540
  115.3 14.6 %all-to-all-start = ((bf16[4,24,2048]{2,1,0:T(8,128)(2,1)}), bf16[4,24,2048]{2,1,0:T(8,128)(2,1)S(1)}, u32[]{:S(2)}, u32[]{:S(2)}) async-start(bf16[4,24,2048]{2,1,0:T(8,128)(2,1)} %get-tuple-element.17), calls=%async_computation | async-start | bytes 786432 | tf_op jit(solution)/shard_map/all_to_all | solution.py:248
  119.0 14.0 %collective-permute-start.12 = (bf16[1,48,2048]{2,1,0:T(8,128)(2,1)S(1)}, bf16[1,48,2048]{2,1,0:T(8,128)(2,1)S(1)}, u32[]{:S(2)}, u32[]{:S(2)}) collective-permute-start(bf16[1,48,2048]{2,1,0:T(8,128)(2,1)S(1)} %bitcast.88), channel_id=1, source_target_pairs={{0,8},{4,12},{8,0},{12,4},{16,24},{20,28},{24,16},{28,20},{1,9},{5... | collective-permute-start | bytes 589832 | tf_op jit(solution)/shard_map/ppermute | solution.py:154
  120.5 13.2 %collective-permute-start.15 = (bf16[1,48,2048]{2,1,0:T(8,128)(2,1)S(1)}, bf16[1,48,2048]{2,1,0:T(8,128)(2,1)S(1)}, u32[]{:S(2)}, u32[]{:S(2)}) collective-permute-start(bf16[1,48,2048]{2,1,0:T(8,128)(2,1)S(1)} %bitcast.80), channel_id=1, source_target_pairs={{0,16},{4,20},{8,24},{12,28},{16,0},{20,4},{24,8},{28,12},{1,17},{... | collective-permute-start | bytes 589832 | tf_op jit(solution)/shard_map/ppermute | solution.py:154
  129.9 11.1 %copy-start.5 = (bf16[16,48,2048]{2,1,0:T(8,128)(2,1)S(1)}, bf16[16,48,2048]{2,1,0:T(8,128)(2,1)}, u32[]{:S(2)}) copy-start(bf16[16,48,2048]{2,1,0:T(8,128)(2,1)} %constant_dynamic-update-slice_fusion.15) | copy-start | bytes 9437188
  130.0 7.7 %collective-permute-start = (bf16[1,48,2048]{2,1,0:T(8,128)(2,1)S(1)}, bf16[1,48,2048]{2,1,0:T(8,128)(2,1)S(1)}, u32[]{:S(2)}, u32[]{:S(2)}) collective-permute-start(bf16[1,48,2048]{2,1,0:T(8,128)(2,1)S(1)} %bitcast.84), channel_id=1, source_target_pairs={{0,8},{4,12},{8,0},{12,4},{16,24},{20,28},{24,16},{28,20},{1,9},{5... | collective-permute-start | bytes 589832 | tf_op jit(solution)/shard_map/ppermute | solution.py:154
  131.5 7.8 %collective-permute-start.3 = (bf16[1,48,2048]{2,1,0:T(8,128)(2,1)S(1)}, bf16[1,48,2048]{2,1,0:T(8,128)(2,1)S(1)}, u32[]{:S(2)}, u32[]{:S(2)}) collective-permute-start(bf16[1,48,2048]{2,1,0:T(8,128)(2,1)S(1)} %bitcast.76), channel_id=1, source_target_pairs={{0,16},{4,20},{8,24},{12,28},{16,0},{20,4},{24,8},{28,12},{1,17},{... | collective-permute-start | bytes 589832 | tf_op jit(solution)/shard_map/ppermute | solution.py:154
  133.0 14.7 %collective-permute-start.13 = (bf16[2,48,2048]{2,1,0:T(8,128)(2,1)S(1)}, bf16[2,48,2048]{2,1,0:T(8,128)(2,1)S(1)}, u32[]{:S(2)}, u32[]{:S(2)}) collective-permute-start(bf16[2,48,2048]{2,1,0:T(8,128)(2,1)S(1)} %pad_maximum_fusion.8), channel_id=1, source_target_pairs={{0,16},{4,20},{8,24},{12,28},{16,0},{20,4},{24,8},{28,12},{1,17},{... | collective-permute-start | bytes 1179656 | tf_op jit(solution)/shard_map/ppermute | solution.py:154
  133.7 14.2 %collective-permute-start.16 = (bf16[2,48,2048]{2,1,0:T(8,128)(2,1)S(1)}, bf16[2,48,2048]{2,1,0:T(8,128)(2,1)S(1)}, u32[]{:S(2)}, u32[]{:S(2)}) collective-permute-start(bf16[2,48,2048]{2,1,0:T(8,128)(2,1)S(1)} %pad_maximum_fusion.9), channel_id=1, source_target_pairs={{0,8},{4,12},{8,0},{12,4},{16,24},{20,28},{24,16},{28,20},{1,9},{5... | collective-permute-start | bytes 1179656 | tf_op jit(solution)/shard_map/ppermute | solution.py:154
  137.8 14.8 %collective-permute-start.1 = (bf16[2,48,2048]{2,1,0:T(8,128)(2,1)S(1)}, bf16[2,48,2048]{2,1,0:T(8,128)(2,1)S(1)}, u32[]{:S(2)}, u32[]{:S(2)}) collective-permute-start(bf16[2,48,2048]{2,1,0:T(8,128)(2,1)S(1)} %pad_maximum_fusion.5), channel_id=1, source_target_pairs={{0,16},{4,20},{8,24},{12,28},{16,0},{20,4},{24,8},{28,12},{1,17},{... | collective-permute-start | bytes 1179656 | tf_op jit(solution)/shard_map/ppermute | solution.py:154
  139.4 13.4 %collective-permute-start.4 = (bf16[2,48,2048]{2,1,0:T(8,128)(2,1)S(1)}, bf16[2,48,2048]{2,1,0:T(8,128)(2,1)S(1)}, u32[]{:S(2)}, u32[]{:S(2)}) collective-permute-start(bf16[2,48,2048]{2,1,0:T(8,128)(2,1)S(1)} %pad_maximum_fusion.6), channel_id=1, source_target_pairs={{0,8},{4,12},{8,0},{12,4},{16,24},{20,28},{24,16},{28,20},{1,9},{5... | collective-permute-start | bytes 1179656 | tf_op jit(solution)/shard_map/ppermute | solution.py:154
  147.8 5.6 %collective-permute-start.14 = (bf16[4,48,2048]{2,1,0:T(8,128)(2,1)S(1)}, bf16[4,48,2048]{2,1,0:T(8,128)(2,1)S(1)}, u32[]{:S(2)}, u32[]{:S(2)}) collective-permute-start(bf16[4,48,2048]{2,1,0:T(8,128)(2,1)S(1)} %pad_maximum_fusion.2), channel_id=1, source_target_pairs={{0,4},{4,0},{8,12},{12,8},{16,20},{20,16},{24,28},{28,24},{1,5},{5... | collective-permute-start | bytes 2359304 | tf_op jit(solution)/shard_map/ppermute | solution.py:154
  148.0 5.6 %collective-permute-start.17 = (bf16[4,48,2048]{2,1,0:T(8,128)(2,1)S(1)}, bf16[4,48,2048]{2,1,0:T(8,128)(2,1)S(1)}, u32[]{:S(2)}, u32[]{:S(2)}) collective-permute-start(bf16[4,48,2048]{2,1,0:T(8,128)(2,1)S(1)} %pad_maximum_fusion.3), channel_id=1, source_target_pairs={{0,4},{4,0},{8,12},{12,8},{16,20},{20,16},{24,28},{28,24},{1,5},{5... | collective-permute-start | bytes 2359304 | tf_op jit(solution)/shard_map/ppermute | solution.py:154
  152.7 16.9 %collective-permute-start.2 = (bf16[4,48,2048]{2,1,0:T(8,128)(2,1)S(1)}, bf16[4,48,2048]{2,1,0:T(8,128)(2,1)S(1)}, u32[]{:S(2)}, u32[]{:S(2)}) collective-permute-start(bf16[4,48,2048]{2,1,0:T(8,128)(2,1)S(1)} %pad_maximum_fusion), channel_id=1, source_target_pairs={{0,4},{4,0},{8,12},{12,8},{16,20},{20,16},{24,28},{28,24},{1,5},{5... | collective-permute-start | bytes 2359304 | tf_op jit(solution)/shard_map/ppermute | solution.py:154
  152.8 16.9 %collective-permute-start.5 = (bf16[4,48,2048]{2,1,0:T(8,128)(2,1)S(1)}, bf16[4,48,2048]{2,1,0:T(8,128)(2,1)S(1)}, u32[]{:S(2)}, u32[]{:S(2)}) collective-permute-start(bf16[4,48,2048]{2,1,0:T(8,128)(2,1)S(1)} %pad_maximum_fusion.1), channel_id=1, source_target_pairs={{0,4},{4,0},{8,12},{12,8},{16,20},{20,16},{24,28},{28,24},{1,5},{5... | collective-permute-start | bytes 2359304 | tf_op jit(solution)/shard_map/ppermute | solution.py:154
  153.6 9.7 %slice-start.3 = ((s8[5767168]{0:T(1024)(128)(4,1)}), s8[4194304]{0:T(1024)(128)(4,1)S(1)}, s32[]{:S(2)}) async-start(s8[5767168]{0:T(1024)(128)(4,1)} %bitcast.105), calls=%async_computation.10 | async-start | bytes 8388608
  153.7 9.6 %slice-start.4 = ((s8[5767168]{0:T(1024)(128)(4,1)}), s8[1572864]{0:T(1024)(128)(4,1)S(1)}, s32[]{:S(2)}) async-start(s8[5767168]{0:T(1024)(128)(4,1)} %bitcast.105), calls=%async_computation.11 | async-start | bytes 3145728
  153.7 16.1 %slice-start = ((s8[11534336]{0:T(1024)(128)(4,1)}), s8[4194304]{0:T(1024)(128)(4,1)S(1)}, s32[]{:S(2)}) async-start(s8[11534336]{0:T(1024)(128)(4,1)} %bitcast.103), calls=%async_computation.7 | async-start | bytes 8388608
  153.8 16.1 %slice-start.1 = ((s8[11534336]{0:T(1024)(128)(4,1)}), s8[4194304]{0:T(1024)(128)(4,1)S(1)}, s32[]{:S(2)}) async-start(s8[11534336]{0:T(1024)(128)(4,1)} %bitcast.103), calls=%async_computation.8 | async-start | bytes 8388608
  163.3 6.6 %slice-start.2 = ((s8[11534336]{0:T(1024)(128)(4,1)}), s8[3145728]{0:T(1024)(128)(4,1)S(1)}, s32[]{:S(2)}) async-start(s8[11534336]{0:T(1024)(128)(4,1)} %bitcast.103), calls=%async_computation.9 | async-start | bytes 6291456
  169.0 13.5 %collective-permute-start.21 = (bf16[4,48,2048]{2,1,0:T(8,128)(2,1)S(1)}, bf16[4,48,2048]{2,1,0:T(8,128)(2,1)S(1)}, u32[]{:S(2)}, u32[]{:S(2)}) collective-permute-start(bf16[4,48,2048]{2,1,0:T(8,128)(2,1)S(1)} %bitcast.97), channel_id=1, source_target_pairs={{0,4},{4,0},{8,12},{12,8},{16,20},{20,16},{24,28},{28,24},{1,5},{5... | collective-permute-start | bytes 2359304 | tf_op jit(solution)/shard_map/ppermute | solution.py:154
  169.1 14.4 %collective-permute-start.18 = (bf16[4,48,2048]{2,1,0:T(8,128)(2,1)S(1)}, bf16[4,48,2048]{2,1,0:T(8,128)(2,1)S(1)}, u32[]{:S(2)}, u32[]{:S(2)}) collective-permute-start(bf16[4,48,2048]{2,1,0:T(8,128)(2,1)S(1)} %bitcast.96), channel_id=1, source_target_pairs={{0,4},{4,0},{8,12},{12,8},{16,20},{20,16},{24,28},{28,24},{1,5},{5... | collective-permute-start | bytes 2359304 | tf_op jit(solution)/shard_map/ppermute | solution.py:154
  182.0 3.3 %collective-permute-start.9 = (bf16[4,48,2048]{2,1,0:T(8,128)(2,1)S(1)}, bf16[4,48,2048]{2,1,0:T(8,128)(2,1)S(1)}, u32[]{:S(2)}, u32[]{:S(2)}) collective-permute-start(bf16[4,48,2048]{2,1,0:T(8,128)(2,1)S(1)} %bitcast.99), channel_id=1, source_target_pairs={{0,4},{4,0},{8,12},{12,8},{16,20},{20,16},{24,28},{28,24},{1,5},{5... | collective-permute-start | bytes 2359304 | tf_op jit(solution)/shard_map/ppermute | solution.py:154
  182.1 5.0 %collective-permute-start.6 = (bf16[4,48,2048]{2,1,0:T(8,128)(2,1)S(1)}, bf16[4,48,2048]{2,1,0:T(8,128)(2,1)S(1)}, u32[]{:S(2)}, u32[]{:S(2)}) collective-permute-start(bf16[4,48,2048]{2,1,0:T(8,128)(2,1)S(1)} %bitcast.98), channel_id=1, source_target_pairs={{0,4},{4,0},{8,12},{12,8},{16,20},{20,16},{24,28},{28,24},{1,5},{5... | collective-permute-start | bytes 2359304 | tf_op jit(solution)/shard_map/ppermute | solution.py:154
  182.9 12.0 %collective-permute-start.22 = (bf16[2,48,2048]{2,1,0:T(8,128)(2,1)S(1)}, bf16[2,48,2048]{2,1,0:T(8,128)(2,1)S(1)}, u32[]{:S(2)}, u32[]{:S(2)}) collective-permute-start(bf16[2,48,2048]{2,1,0:T(8,128)(2,1)S(1)} %slice.255), channel_id=1, source_target_pairs={{0,8},{4,12},{8,0},{12,4},{16,24},{20,28},{24,16},{28,20},{1,9},{5... | collective-permute-start | bytes 1179656 | tf_op jit(solution)/shard_map/ppermute | solution.py:154
  183.8 12.7 %collective-permute-start.19 = (bf16[2,48,2048]{2,1,0:T(8,128)(2,1)S(1)}, bf16[2,48,2048]{2,1,0:T(8,128)(2,1)S(1)}, u32[]{:S(2)}, u32[]{:S(2)}) collective-permute-start(bf16[2,48,2048]{2,1,0:T(8,128)(2,1)S(1)} %slice.249), channel_id=1, source_target_pairs={{0,16},{4,20},{8,24},{12,28},{16,0},{20,4},{24,8},{28,12},{1,17},{... | collective-permute-start | bytes 1179656 | tf_op jit(solution)/shard_map/ppermute | solution.py:154
  185.6 17.7 %collective-permute-start.10 = (bf16[2,48,2048]{2,1,0:T(8,128)(2,1)S(1)}, bf16[2,48,2048]{2,1,0:T(8,128)(2,1)S(1)}, u32[]{:S(2)}, u32[]{:S(2)}) collective-permute-start(bf16[2,48,2048]{2,1,0:T(8,128)(2,1)S(1)} %slice.238), channel_id=1, source_target_pairs={{0,8},{4,12},{8,0},{12,4},{16,24},{20,28},{24,16},{28,20},{1,9},{5... | collective-permute-start | bytes 1179656 | tf_op jit(solution)/shard_map/ppermute | solution.py:154
  187.5 17.5 %collective-permute-start.7 = (bf16[2,48,2048]{2,1,0:T(8,128)(2,1)S(1)}, bf16[2,48,2048]{2,1,0:T(8,128)(2,1)S(1)}, u32[]{:S(2)}, u32[]{:S(2)}) collective-permute-start(bf16[2,48,2048]{2,1,0:T(8,128)(2,1)S(1)} %slice.232), channel_id=1, source_target_pairs={{0,16},{4,20},{8,24},{12,28},{16,0},{20,4},{24,8},{28,12},{1,17},{... | collective-permute-start | bytes 1179656 | tf_op jit(solution)/shard_map/ppermute | solution.py:154
  195.0 13.5 %collective-permute-start.23 = (bf16[1,48,2048]{2,1,0:T(8,128)(2,1)S(1)}, bf16[1,48,2048]{2,1,0:T(8,128)(2,1)S(1)}, u32[]{:S(2)}, u32[]{:S(2)}) collective-permute-start(bf16[1,48,2048]{2,1,0:T(8,128)(2,1)S(1)} %slice.257), channel_id=1, source_target_pairs={{0,16},{4,20},{8,24},{12,28},{16,0},{20,4},{24,8},{28,12},{1,17},{... | collective-permute-start | bytes 589832 | tf_op jit(solution)/shard_map/ppermute | solution.py:154
  196.7 11.9 %collective-permute-start.20 = (bf16[1,48,2048]{2,1,0:T(8,128)(2,1)S(1)}, bf16[1,48,2048]{2,1,0:T(8,128)(2,1)S(1)}, u32[]{:S(2)}, u32[]{:S(2)}) collective-permute-start(bf16[1,48,2048]{2,1,0:T(8,128)(2,1)S(1)} %slice.251), channel_id=1, source_target_pairs={{0,8},{4,12},{8,0},{12,4},{16,24},{20,28},{24,16},{28,20},{1,9},{5... | collective-permute-start | bytes 589832 | tf_op jit(solution)/shard_map/ppermute | solution.py:154
  203.4 9.7 %collective-permute-start.11 = (bf16[1,48,2048]{2,1,0:T(8,128)(2,1)S(1)}, bf16[1,48,2048]{2,1,0:T(8,128)(2,1)S(1)}, u32[]{:S(2)}, u32[]{:S(2)}) collective-permute-start(bf16[1,48,2048]{2,1,0:T(8,128)(2,1)S(1)} %slice.240), channel_id=1, source_target_pairs={{0,16},{4,20},{8,24},{12,28},{16,0},{20,4},{24,8},{28,12},{1,17},{... | collective-permute-start | bytes 589832 | tf_op jit(solution)/shard_map/ppermute | solution.py:154
  205.1 8.2 %collective-permute-start.8 = (bf16[1,48,2048]{2,1,0:T(8,128)(2,1)S(1)}, bf16[1,48,2048]{2,1,0:T(8,128)(2,1)S(1)}, u32[]{:S(2)}, u32[]{:S(2)}) collective-permute-start(bf16[1,48,2048]{2,1,0:T(8,128)(2,1)S(1)} %slice.234), channel_id=1, source_target_pairs={{0,8},{4,12},{8,0},{12,4},{16,24},{20,28},{24,16},{28,20},{1,9},{5... | collective-permute-start | bytes 589832 | tf_op jit(solution)/shard_map/ppermute | solution.py:154
  209.4 27.7 %copy-start.1 = (f32[2048,8]{0,1:T(8,128)S(1)}, f32[2048,8]{0,1:T(8,128)}, u32[]{:S(2)}) copy-start(f32[2048,8]{0,1:T(8,128)} %param.19) | copy-start | bytes 196612
  209.4 13.4 %all-to-all-start.3 = ((bf16[4,24,2048]{2,1,0:T(8,128)(2,1)}), bf16[4,24,2048]{2,1,0:T(8,128)(2,1)S(1)}, u32[]{:S(2)}, u32[]{:S(2)}) async-start(bf16[4,24,2048]{2,1,0:T(8,128)(2,1)} %bitcast.30), calls=%async_computation.3 | async-start | bytes 786432 | tf_op jit(solution)/shard_map/all_to_all | solution.py:264
  222.8 13.0 %all-to-all-start.1 = ((bf16[4,24,2048]{2,1,0:T(8,128)(2,1)}), bf16[4,24,2048]{2,1,0:T(8,128)(2,1)S(1)}, u32[]{:S(2)}, u32[]{:S(2)}) async-start(bf16[4,24,2048]{2,1,0:T(8,128)(2,1)} %bitcast.16), calls=%async_computation.1 | async-start | bytes 786432 | tf_op jit(solution)/shard_map/all_to_all | solution.py:264
Sparse Core Ops, SparseCore 0:
  11.4 31.6 all-gather.1
  71.3 26.5 reduce-scatter.3

commit v3 on v2

--- a/solution.py
+++ b/solution.py
@@ -149,22 +149,28 @@
     )(rows, info, table, w_key, w_value, w_query, w_out)
 
 
-def exchange(values, step):
-    pairs = [(i, i ^ step) for i in range(lax.axis_size("req"))]
-    return lax.ppermute(values, "req", pairs)
-
-
-def spread(block, order):
+def exchange(values, step, axis):
+    pairs = [(i, i ^ step) for i in range(lax.axis_size(axis))]
+    return lax.ppermute(values, axis, pairs)
+
+
+def shuffled(stack, places):
+    return jnp.concatenate(
+        [lax.dynamic_index_in_dim(stack, place, 0, keepdims=True) for place in places], axis=0
+    )
+
+
+def spread(block, order, axis="req"):
     stack = block[None]
     for step in order:
-        stack = jnp.concatenate([stack, exchange(stack, step)], axis=0)
+        stack = jnp.concatenate([stack, exchange(stack, step, axis)], axis=0)
     return stack
 
 
-def collect(stack, order):
+def collect(stack, order, axis="req"):
     for step in order[::-1]:
         kept = stack.shape[0] // 2
-        arrived = exchange(stack[kept:], step)
+        arrived = exchange(stack[kept:], step, axis)
         stack = (stack[:kept].astype(jnp.float32) + arrived.astype(jnp.float32)).astype(
             jnp.bfloat16
         )
@@ -196,9 +202,16 @@
         [attn_routes, segment_ids.reshape(row_count, 1), jnp.zeros((row_count, 125), jnp.int32)],
         axis=1,
     ).astype(jnp.bfloat16)
-    gathered = lax.all_gather(
-        jnp.concatenate([normed, labels], axis=1), "head", axis=0, tiled=True
-    )
+    head_order = [1 << bit for bit in range(head_count.bit_length() - 1)][::-1]
+    masks = [0]
+    for step in head_order:
+        masks = masks + [mask | step for mask in masks]
+    head_index = lax.axis_index("head")
+    held_at = jnp.array([masks.index(mask) for mask in range(head_count)], jnp.int32)
+    stack = spread(jnp.concatenate([normed, labels], axis=1), head_order, "head")
+    gathered = shuffled(
+        stack, [held_at[head_index ^ place] for place in range(head_count)]
+    ).reshape(seq_length, -1)
     normed_all = gathered[:, :D]
     labels_all = gathered[:, D : D + 3].astype(jnp.int32)
     routes_all, segment_row = labels_all[:, :2], labels_all[:, 2]
@@ -216,8 +229,9 @@
     partial_value = attention(
         normed_all, info, table, w_key, w_value, w_query, w_out, capacity
     )
-    attn_rows = lax.psum_scatter(
-        partial_value, "head", scatter_dimension=0, tiled=True
+    blocks = partial_value.reshape(head_count, row_count, D)
+    attn_rows = collect(
+        shuffled(blocks, [head_index ^ mask for mask in masks]), head_order, "head"
     ).astype(jnp.float32)
     residual = (hidden_in.astype(jnp.float32) + attn_rows).astype(jnp.bfloat16)
     ffn_normed = rms_norm(residual, ffn_gain)

time: 245 us -> 229 us (0.935)
  waiting for transfers between devices: 113 us -> 91.8 us
  starting transfers between devices: 32.8 us -> 43.7 us
  between operations: 14.1 us -> 8.37 us
    ppermute x24 -> x28, waiting for transfers between devices: 29.3 us -> 67.2 us  [exchange(): return lax.ppermute(values, axis, pairs)]
    all_gather x1 -> x0, waiting for transfers between devices: 31.7 us -> none  [per_device(): lax.all_gather(jnp.concatenate([normed, labels], axis=1), 'head', axis=0,...]
    reduce_scatter x1 -> x0, waiting for transfers between devices: 26.8 us -> none  [per_device(): lax.psum_scatter(partial_value, 'head', scatter_dimension=0, tiled=True)]
    ppermute x24 -> x28, starting transfers between devices: 21.9 us -> 32.2 us  [exchange(): return lax.ppermute(values, axis, pairs)]
  transfers between devices with their start and end apart: 29 -> 31, of which waited for: 12 -> 13; matrix products, arithmetic and copies ran while one was open for 13% -> 15% of each run, Pallas kernels for 0% -> 0%
where the time goes in v3:
time: 229 us
  waiting for transfers between devices  91.8 us (40%)
  starting transfers between devices  43.7 us (19%)
  matrix products  31.2 us (14%)
  Pallas kernels  22.4 us (10%)
  blocking collectives  15.7 us (7%)
  other arithmetic  9.46 us (4%)
  between operations  8.37 us (4%)
  local copies, waits for them, and re-layouts  6.04 us (3%)
    ppermute x28, waiting for transfers between devices, exchange(): return lax.ppermute(values, axis, pairs)  67.2 us
    ppermute x28, starting transfers between devices, exchange(): return lax.ppermute(values, axis, pairs)  32.2 us
    pallas_call x1, Pallas kernels, attention(): pl.pallas_call(functools.partial(attention_kernel, capacity), grid=(E_ATT...  22.4 us
    all_to_all x2, waiting for transfers between devices, per_device(): lax.all_to_all(summed.reshape(head_count, cap_ffn, D), 'head', split_axis...  18.1 us
    dot_general x2, matrix products, per_device(): jnp.einsum('md,dgf->mgf', rows, w_gate_up[expert], preferred_element_type...  15.8 us
    all_to_all x1, blocking collectives, per_device(): lax.all_to_all(outgoing[:, expert], 'head', split_axis=0, concat_axis=0,...  15.7 us
    dot_general x2, matrix products, per_device(): jnp.dot(activated, w_down[expert], preferred_element_type=jnp.float32)  11 us
    all_to_all x2, starting transfers between devices, per_device(): lax.all_to_all(summed.reshape(head_count, cap_ffn, D), 'head', split_axis...  7.86 us
  transfers between devices with their start and end apart: 31, of which 13 were waited for; matrix products, arithmetic and copies ran while one was open for 15% of the time, Pallas kernels for 0%

profile of v3, /device:TPU:0, one launch (start us, length us, event | category | flops | bytes accessed | tf_op | source)
XLA Modules:
  0.0 228.6 jit_solution(15415742515494274062)
XLA Ops:
  0.0 1.1 fusion.21
  1.2 0.7 convert.14
  2.0 0.7 convert_bitcast_fusion
  2.7 1.1 fusion.23
  3.9 4.1 %collective-permute-start = (bf16[1,64,2176]{2,1,0:T(8,128)(2,1)S(1)}, bf16[1,64,2176]{2,1,0:T(8,128)(2,1)S(1)}, u32[]{:S(2)}, u32[]{:S(2)}) collective-permute-start(bf16[1,64,2176]{2,1,0:T(8,128)(2,1)S(1)} %bitcast.110), channel_id=1, source_target_pairs={{0,2},{1,3},{2,0},{3,1},{4,6},{5,7},{6,4},{7,5},{8,10},{9,11},{10,... | collective-permute-start | bytes 835592 | tf_op jit(solution)/shard_map/ppermute | solution.py:154
  8.0 12.6 %collective-permute-done = bf16[1,64,2176]{2,1,0:T(8,128)(2,1)S(1)} collective-permute-done((bf16[1,64,2176]{2,1,0:T(8,128)(2,1)S(1)}, bf16[1,64,2176]{2,1,0:T(8,128)(2,1)S(1)}, u32[]{:S(2)}, u32[]{:S(2)}) %collective-permute-start) | collective-permute-done | bytes 278560 | tf_op jit(solution)/shard_map/ppermute | solution.py:154
  20.7 0.8 collective-permute-start.1
  21.5 1.4 fusion.44
  30.6 4.0 %collective-permute-done.1 = bf16[2,64,2176]{2,1,0:T(8,128)(2,1)S(1)} collective-permute-done((bf16[2,64,2176]{2,1,0:T(8,128)(2,1)S(1)}, bf16[2,64,2176]{2,1,0:T(8,128)(2,1)S(1)}, u32[]{:S(2)}, u32[]{:S(2)}) %collective-permute-start.1) | collective-permute-done | bytes 557088 | tf_op jit(solution)/shard_map/ppermute | solution.py:154
  35.2 0.9 copy-done.3
  36.2 2.1 fusion.36
  38.7 0.5 multiply_cosine_fusion
  39.5 22.4 %shard_map.145 = bf16[256,2048]{1,0:T(8,128)(2,1)S(1)} custom-call(bf16[256,2048]{1,0:T(8,128)(2,1)S(1)} %slice.232.rows_ref, f32[8,256]{1,0:T(8,128)S(1)} %maximum_bitcast_fusion.info_ref, f32[256,256]{1,0:T(8,128)S(1)} %pad_maximum_fusion.15.table_ref, bf16[2048,512]{1,0:T(8,128)(2,1)S(1)} %copy-done.2, bf16[2048,512]{1,0:T(8,128)(2,1)} %w_value_ref.1, ...), custom_call_target="tpu_custom_call" | custom-call | flops 12000000000 | bytes 40000000 | tf_op jit(solution)/shard_map/pallas_call | solution.py:126
  62.1 1.5 collective-permute-start.2
  63.6 11.3 %collective-permute-done.2 = bf16[2,64,2048]{2,1,0:T(8,128)(2,1)S(1)} collective-permute-done((bf16[2,64,2048]{2,1,0:T(8,128)(2,1)S(1)}, bf16[2,64,2048]{2,1,0:T(8,128)(2,1)S(1)}, u32[]{:S(2)}, u32[]{:S(2)}) %collective-permute-start.2) | collective-permute-done | bytes 524320 | tf_op jit(solution)/shard_map/ppermute | solution.py:154
  75.1 3.8 %collective-permute-start.3 = (bf16[1,64,2048]{2,1,0:T(8,128)(2,1)S(1)}, bf16[1,64,2048]{2,1,0:T(8,128)(2,1)S(1)}, u32[]{:S(2)}, u32[]{:S(2)}) collective-permute-start(bf16[1,64,2048]{2,1,0:T(8,128)(2,1)S(1)} %slice.237), channel_id=1, source_target_pairs={{0,2},{1,3},{2,0},{3,1},{4,6},{5,7},{6,4},{7,5},{8,10},{9,11},{10,... | collective-permute-start | bytes 786440 | tf_op jit(solution)/shard_map/ppermute | solution.py:154
  78.8 10.6 %collective-permute-done.3 = bf16[1,64,2048]{2,1,0:T(8,128)(2,1)S(1)} collective-permute-done((bf16[1,64,2048]{2,1,0:T(8,128)(2,1)S(1)}, bf16[1,64,2048]{2,1,0:T(8,128)(2,1)S(1)}, u32[]{:S(2)}, u32[]{:S(2)}) %collective-permute-start.3) | collective-permute-done | bytes 262176 | tf_op jit(solution)/shard_map/ppermute | solution.py:154
  89.7 0.4 fusion.31
  90.4 0.4 convolution_convert_fusion.2
  90.9 0.8 slice_bitcast_fusion.1
  91.7 15.7 %all_to_all.20 = bf16[4,24,2048]{2,1,0:T(8,128)(2,1)S(1)} all-to-all(bf16[4,24,2048]{2,1,0:T(8,128)(2,1)S(1)} %get-tuple-element.26), channel_id=1, replica_groups=mesh['req'=8,'head'=4] {'head'}, dimensions={0} | all-to-all | bytes 786432 | tf_op jit(solution)/shard_map/all_to_all | solution.py:262
  107.4 3.6 %all-to-all-start = ((bf16[4,24,2048]{2,1,0:T(8,128)(2,1)}), bf16[4,24,2048]{2,1,0:T(8,128)(2,1)S(1)}, u32[]{:S(2)}, u32[]{:S(2)}) async-start(bf16[4,24,2048]{2,1,0:T(8,128)(2,1)} %get-tuple-element.25), calls=%async_computation | async-start | bytes 786432 | tf_op jit(solution)/shard_map/all_to_all | solution.py:262
  111.1 1.6 collective-permute-start.16
  112.6 1.5 collective-permute-start.19
  114.1 0.7 constant_dynamic-update-slice_fusion.15
  114.8 6.5 %all-to-all-done = bf16[4,24,2048]{2,1,0:T(8,128)(2,1)S(1)} async-done(((bf16[4,24,2048]{2,1,0:T(8,128)(2,1)}), bf16[4,24,2048]{2,1,0:T(8,128)(2,1)S(1)}, u32[]{:S(2)}, u32[]{:S(2)}) %all-to-all-start) | async-done | bytes 393248 | tf_op jit(solution)/shard_map/all_to_all | solution.py:262
  121.4 1.6 collective-permute-start.4
  122.9 1.5 collective-permute-start.7
  124.5 0.6 collective-permute-start.17
  125.1 0.6 collective-permute-start.20
  125.7 3.4 %collective-permute-done.4 = bf16[1,48,2048]{2,1,0:T(8,128)(2,1)S(1)} collective-permute-done((bf16[1,48,2048]{2,1,0:T(8,128)(2,1)S(1)}, bf16[1,48,2048]{2,1,0:T(8,128)(2,1)S(1)}, u32[]{:S(2)}, u32[]{:S(2)}) %collective-permute-start.4) | collective-permute-done | bytes 196640 | tf_op jit(solution)/shard_map/ppermute | solution.py:154
  129.2 1.6 collective-permute-start.5
  130.9 1.6 collective-permute-start.8
  132.5 6.6 %collective-permute-done.17 = bf16[2,48,2048]{2,1,0:T(8,128)(2,1)S(1)} collective-permute-done((bf16[2,48,2048]{2,1,0:T(8,128)(2,1)S(1)}, bf16[2,48,2048]{2,1,0:T(8,128)(2,1)S(1)}, u32[]{:S(2)}, u32[]{:S(2)}) %collective-permute-start.17) | collective-permute-done | bytes 393248 | tf_op jit(solution)/shard_map/ppermute | solution.py:154
  139.4 0.5 collective-permute-start.21
  140.0 3.5 %collective-permute-done.5 = bf16[2,48,2048]{2,1,0:T(8,128)(2,1)S(1)} collective-permute-done((bf16[2,48,2048]{2,1,0:T(8,128)(2,1)S(1)}, bf16[2,48,2048]{2,1,0:T(8,128)(2,1)S(1)}, u32[]{:S(2)}, u32[]{:S(2)}) %collective-permute-start.5) | collective-permute-done | bytes 393248 | tf_op jit(solution)/shard_map/ppermute | solution.py:154
  143.7 0.5 collective-permute-start.9
  144.6 9.5 %fusion = f32[768,2,704]{0,2,1:T(8,128)} fusion(bf16[768,2048,1]{1,0,2:T(8,128)(2,1)S(1)} %bitcast.119, bf16[2,2048,2,704]{1,3,2,0:T(8,128)(2,1)} %param.27), kind=kOutput, calls=%fused_computation | convolution fusion | flops 4429185024 | bytes 13238272 | tf_op jit(solution)/shard_map/md,dgf->mgf/dot_general | solution.py:267
  154.2 5.5 %convolution_convert_fusion = bf16[768,2048]{1,0:T(8,128)(2,1)S(1)} fusion(bf16[2,704,2048]{2,1,0:T(8,128)(2,1)S(1)} %bitcast.125, f32[768,2,704]{0,2,1:T(8,128)} %fusion), kind=kOutput, calls=%fused_computation.6 | convolution fusion | flops 2219409408 | bytes 10354688 | tf_op jit(solution)/shard_map/dot_general | solution.py:272
  160.0 0.5 collective-permute-start.22
  160.8 6.3 %fusion.2 = f32[768,2,704]{0,2,1:T(8,128)} fusion(bf16[768,2048,1]{1,0,2:T(8,128)(2,1)S(1)} %bitcast.120, bf16[2,2048,2,704]{1,3,2,0:T(8,128)(2,1)S(1)} %bitcast.123), kind=kOutput, calls=%fused_computation.2 | convolution fusion | flops 4429185024 | bytes 13238272 | tf_op jit(solution)/shard_map/md,dgf->mgf/dot_general | solution.py:267
  167.1 5.5 %convolution_convert_fusion.1 = bf16[768,2048]{1,0:T(8,128)(2,1)S(1)} fusion(bf16[2,704,2048]{2,1,0:T(8,128)(2,1)S(1)} %bitcast.125, f32[768,2,704]{0,2,1:T(8,128)} %fusion.2), kind=kOutput, calls=%fused_computation.7 | convolution fusion | flops 2219409408 | bytes 10354688 | tf_op jit(solution)/shard_map/dot_general | solution.py:272
  173.0 0.4 collective-permute-start.10
  173.4 0.3 fusion.13
  173.7 0.6 collective-permute-start.26
  174.3 0.3 fusion.14
  174.6 1.6 collective-permute-start.23
  176.5 1.6 collective-permute-start.14
  178.1 0.3 fusion.16
  178.4 0.6 collective-permute-start.11
  179.0 6.8 %collective-permute-done.26 = bf16[2,48,2048]{2,1,0:T(8,128)(2,1)S(1)} collective-permute-done((bf16[2,48,2048]{2,1,0:T(8,128)(2,1)S(1)}, bf16[2,48,2048]{2,1,0:T(8,128)(2,1)S(1)}, u32[]{:S(2)}, u32[]{:S(2)}) %collective-permute-start.26) | collective-permute-done | bytes 393248 | tf_op jit(solution)/shard_map/ppermute | solution.py:154
  185.9 1.6 collective-permute-start.27
  187.6 0.8 collective-permute-start.24
  188.4 5.8 %collective-permute-done.14 = bf16[2,48,2048]{2,1,0:T(8,128)(2,1)S(1)} collective-permute-done((bf16[2,48,2048]{2,1,0:T(8,128)(2,1)S(1)}, bf16[2,48,2048]{2,1,0:T(8,128)(2,1)S(1)}, u32[]{:S(2)}, u32[]{:S(2)}) %collective-permute-start.14) | collective-permute-done | bytes 393248 | tf_op jit(solution)/shard_map/ppermute | solution.py:154
  194.3 1.6 collective-permute-start.15
  196.0 0.8 collective-permute-start.12
  196.8 2.5 %collective-permute-done.27 = bf16[1,48,2048]{2,1,0:T(8,128)(2,1)S(1)} collective-permute-done((bf16[1,48,2048]{2,1,0:T(8,128)(2,1)S(1)}, bf16[1,48,2048]{2,1,0:T(8,128)(2,1)S(1)}, u32[]{:S(2)}, u32[]{:S(2)}) %collective-permute-start.27) | collective-permute-done | bytes 196640 | tf_op jit(solution)/shard_map/ppermute | solution.py:154
  199.5 0.8 pad_maximum_fusion.14
  200.3 4.4 %all-to-all-start.3 = ((bf16[4,24,2048]{2,1,0:T(8,128)(2,1)}), bf16[4,24,2048]{2,1,0:T(8,128)(2,1)S(1)}, u32[]{:S(2)}, u32[]{:S(2)}) async-start(bf16[4,24,2048]{2,1,0:T(8,128)(2,1)} %bitcast.38), calls=%async_computation.3 | async-start | bytes 786432 | tf_op jit(solution)/shard_map/all_to_all | solution.py:278
  204.8 0.8 pad_maximum_fusion.11
  205.6 8.7 %all-to-all-done.3 = bf16[4,24,2048]{2,1,0:T(8,128)(2,1)S(1)} async-done(((bf16[4,24,2048]{2,1,0:T(8,128)(2,1)}), bf16[4,24,2048]{2,1,0:T(8,128)(2,1)S(1)}, u32[]{:S(2)}, u32[]{:S(2)}) %all-to-all-start.3) | async-done | bytes 393248 | tf_op jit(solution)/shard_map/all_to_all | solution.py:278
  214.3 3.5 %all-to-all-start.1 = ((bf16[4,24,2048]{2,1,0:T(8,128)(2,1)}), bf16[4,24,2048]{2,1,0:T(8,128)(2,1)S(1)}, u32[]{:S(2)}, u32[]{:S(2)}) async-start(bf16[4,24,2048]{2,1,0:T(8,128)(2,1)} %bitcast.24), calls=%async_computation.1 | async-start | bytes 786432 | tf_op jit(solution)/shard_map/all_to_all | solution.py:278
  217.9 9.4 %all-to-all-done.1 = bf16[4,24,2048]{2,1,0:T(8,128)(2,1)S(1)} async-done(((bf16[4,24,2048]{2,1,0:T(8,128)(2,1)}), bf16[4,24,2048]{2,1,0:T(8,128)(2,1)S(1)}, u32[]{:S(2)}, u32[]{:S(2)}) %all-to-all-start.1) | async-done | bytes 393248 | tf_op jit(solution)/shard_map/all_to_all | solution.py:278
  227.4 1.2 fusion.10
  (135 shorter events, 5.7 us)
Async XLA Ops:
  0.0 36.2 %copy-start = (f32[2048,8]{0,1:T(8,128)S(1)}, f32[2048,8]{0,1:T(8,128)}, u32[]{:S(2)}) copy-start(f32[2048,8]{0,1:T(8,128)} %param.20) | copy-start | bytes 196612
  3.9 16.7 %collective-permute-start = (bf16[1,64,2176]{2,1,0:T(8,128)(2,1)S(1)}, bf16[1,64,2176]{2,1,0:T(8,128)(2,1)S(1)}, u32[]{:S(2)}, u32[]{:S(2)}) collective-permute-start(bf16[1,64,2176]{2,1,0:T(8,128)(2,1)S(1)} %bitcast.110), channel_id=1, source_target_pairs={{0,2},{1,3},{2,0},{3,1},{4,6},{5,7},{6,4},{7,5},{8,10},{9,11},{10,... | collective-permute-start | bytes 835592 | tf_op jit(solution)/shard_map/ppermute | solution.py:154
  20.7 13.9 %collective-permute-start.1 = (bf16[2,64,2176]{2,1,0:T(8,128)(2,1)S(1)}, bf16[2,64,2176]{2,1,0:T(8,128)(2,1)S(1)}, u32[]{:S(2)}, u32[]{:S(2)}) collective-permute-start(bf16[2,64,2176]{2,1,0:T(8,128)(2,1)S(1)} %pad_maximum_fusion.7), channel_id=1, source_target_pairs={{0,1},{1,0},{2,3},{3,2},{4,5},{5,4},{6,7},{7,6},{8,9},{9,8},{10,11... | collective-permute-start | bytes 1671176 | tf_op jit(solution)/shard_map/ppermute | solution.py:154
  34.9 4.6 %copy-start.2 = (bf16[2048,512]{1,0:T(8,128)(2,1)S(1)}, bf16[2048,512]{1,0:T(8,128)(2,1)}, u32[]{:S(2)}) copy-start(bf16[2048,512]{1,0:T(8,128)(2,1)} %w_key_ref.1) | copy-start | bytes 6291460
  35.0 1.0 copy-start.3
  61.9 27.6 %copy-start.4 = (bf16[64,2048]{1,0:T(8,128)(2,1)S(1)}, bf16[64,2048]{1,0:T(8,128)(2,1)}, u32[]{:S(2)}) copy-start(bf16[64,2048]{1,0:T(8,128)(2,1)} %param.15) | copy-start | bytes 786436
  61.9 27.8 %copy-start.7 = (f32[2048]{0:T(1024)S(1)}, f32[2048]{0:T(1024)}, u32[]{:S(2)}) copy-start(f32[2048]{0:T(1024)} %param.25) | copy-start | bytes 24580
  61.9 27.8 %copy-start.8 = (f32[2048,8]{0,1:T(8,128)S(1)}, f32[2048,8]{0,1:T(8,128)}, u32[]{:S(2)}) copy-start(f32[2048,8]{0,1:T(8,128)} %param.26) | copy-start | bytes 196612
  61.9 28.2 %copy-start.6 = (s32[64,2]{0,1:T(2,128)S(1)}, s32[64,2]{0,1:T(2,128)}, u32[]{:S(2)}) copy-start(s32[64,2]{0,1:T(2,128)} %param.18) | copy-start | bytes 1540
  62.1 12.8 %collective-permute-start.2 = (bf16[2,64,2048]{2,1,0:T(8,128)(2,1)S(1)}, bf16[2,64,2048]{2,1,0:T(8,128)(2,1)S(1)}, u32[]{:S(2)}, u32[]{:S(2)}) collective-permute-start(bf16[2,64,2048]{2,1,0:T(8,128)(2,1)S(1)} %pad_maximum_fusion.8), channel_id=1, source_target_pairs={{0,1},{1,0},{2,3},{3,2},{4,5},{5,4},{6,7},{7,6},{8,9},{9,8},{10,11... | collective-permute-start | bytes 1572872 | tf_op jit(solution)/shard_map/ppermute | solution.py:154
  75.1 14.4 %collective-permute-start.3 = (bf16[1,64,2048]{2,1,0:T(8,128)(2,1)S(1)}, bf16[1,64,2048]{2,1,0:T(8,128)(2,1)S(1)}, u32[]{:S(2)}, u32[]{:S(2)}) collective-permute-start(bf16[1,64,2048]{2,1,0:T(8,128)(2,1)S(1)} %slice.237), channel_id=1, source_target_pairs={{0,2},{1,3},{2,0},{3,1},{4,6},{5,7},{6,4},{7,5},{8,10},{9,11},{10,... | collective-permute-start | bytes 786440 | tf_op jit(solution)/shard_map/ppermute | solution.py:154
  107.4 13.9 %all-to-all-start = ((bf16[4,24,2048]{2,1,0:T(8,128)(2,1)}), bf16[4,24,2048]{2,1,0:T(8,128)(2,1)S(1)}, u32[]{:S(2)}, u32[]{:S(2)}) async-start(bf16[4,24,2048]{2,1,0:T(8,128)(2,1)} %get-tuple-element.25), calls=%async_computation | async-start | bytes 786432 | tf_op jit(solution)/shard_map/all_to_all | solution.py:262
  111.1 13.4 %collective-permute-start.16 = (bf16[1,48,2048]{2,1,0:T(8,128)(2,1)S(1)}, bf16[1,48,2048]{2,1,0:T(8,128)(2,1)S(1)}, u32[]{:S(2)}, u32[]{:S(2)}) collective-permute-start(bf16[1,48,2048]{2,1,0:T(8,128)(2,1)S(1)} %bitcast.104), channel_id=1, source_target_pairs={{0,8},{4,12},{8,0},{12,4},{16,24},{20,28},{24,16},{28,20},{1,9},{5... | collective-permute-start | bytes 589832 | tf_op jit(solution)/shard_map/ppermute | solution.py:154
  112.6 12.5 %collective-permute-start.19 = (bf16[1,48,2048]{2,1,0:T(8,128)(2,1)S(1)}, bf16[1,48,2048]{2,1,0:T(8,128)(2,1)S(1)}, u32[]{:S(2)}, u32[]{:S(2)}) collective-permute-start(bf16[1,48,2048]{2,1,0:T(8,128)(2,1)S(1)} %bitcast.96), channel_id=1, source_target_pairs={{0,16},{4,20},{8,24},{12,28},{16,0},{20,4},{24,8},{28,12},{1,17},{... | collective-permute-start | bytes 589832 | tf_op jit(solution)/shard_map/ppermute | solution.py:154
  121.3 11.2 %copy-start.5 = (bf16[16,48,2048]{2,1,0:T(8,128)(2,1)S(1)}, bf16[16,48,2048]{2,1,0:T(8,128)(2,1)}, u32[]{:S(2)}) copy-start(bf16[16,48,2048]{2,1,0:T(8,128)(2,1)} %constant_dynamic-update-slice_fusion.15) | copy-start | bytes 9437188
  121.4 7.8 %collective-permute-start.4 = (bf16[1,48,2048]{2,1,0:T(8,128)(2,1)S(1)}, bf16[1,48,2048]{2,1,0:T(8,128)(2,1)S(1)}, u32[]{:S(2)}, u32[]{:S(2)}) collective-permute-start(bf16[1,48,2048]{2,1,0:T(8,128)(2,1)S(1)} %bitcast.100), channel_id=1, source_target_pairs={{0,8},{4,12},{8,0},{12,4},{16,24},{20,28},{24,16},{28,20},{1,9},{5... | collective-permute-start | bytes 589832 | tf_op jit(solution)/shard_map/ppermute | solution.py:154
  122.9 7.9 %collective-permute-start.7 = (bf16[1,48,2048]{2,1,0:T(8,128)(2,1)S(1)}, bf16[1,48,2048]{2,1,0:T(8,128)(2,1)S(1)}, u32[]{:S(2)}, u32[]{:S(2)}) collective-permute-start(bf16[1,48,2048]{2,1,0:T(8,128)(2,1)S(1)} %bitcast.92), channel_id=1, source_target_pairs={{0,16},{4,20},{8,24},{12,28},{16,0},{20,4},{24,8},{28,12},{1,17},{... | collective-permute-start | bytes 589832 | tf_op jit(solution)/shard_map/ppermute | solution.py:154
  124.5 14.7 %collective-permute-start.17 = (bf16[2,48,2048]{2,1,0:T(8,128)(2,1)S(1)}, bf16[2,48,2048]{2,1,0:T(8,128)(2,1)S(1)}, u32[]{:S(2)}, u32[]{:S(2)}) collective-permute-start(bf16[2,48,2048]{2,1,0:T(8,128)(2,1)S(1)} %pad_maximum_fusion.12), channel_id=1, source_target_pairs={{0,16},{4,20},{8,24},{12,28},{16,0},{20,4},{24,8},{28,12},{1,17},{... | collective-permute-start | bytes 1179656 | tf_op jit(solution)/shard_map/ppermute | solution.py:154
  125.1 14.2 %collective-permute-start.20 = (bf16[2,48,2048]{2,1,0:T(8,128)(2,1)S(1)}, bf16[2,48,2048]{2,1,0:T(8,128)(2,1)S(1)}, u32[]{:S(2)}, u32[]{:S(2)}) collective-permute-start(bf16[2,48,2048]{2,1,0:T(8,128)(2,1)S(1)} %pad_maximum_fusion.13), channel_id=1, source_target_pairs={{0,8},{4,12},{8,0},{12,4},{16,24},{20,28},{24,16},{28,20},{1,9},{5... | collective-permute-start | bytes 1179656 | tf_op jit(solution)/shard_map/ppermute | solution.py:154
  129.2 14.2 %collective-permute-start.5 = (bf16[2,48,2048]{2,1,0:T(8,128)(2,1)S(1)}, bf16[2,48,2048]{2,1,0:T(8,128)(2,1)S(1)}, u32[]{:S(2)}, u32[]{:S(2)}) collective-permute-start(bf16[2,48,2048]{2,1,0:T(8,128)(2,1)S(1)} %pad_maximum_fusion.9), channel_id=1, source_target_pairs={{0,16},{4,20},{8,24},{12,28},{16,0},{20,4},{24,8},{28,12},{1,17},{... | collective-permute-start | bytes 1179656 | tf_op jit(solution)/shard_map/ppermute | solution.py:154
  130.9 12.8 %collective-permute-start.8 = (bf16[2,48,2048]{2,1,0:T(8,128)(2,1)S(1)}, bf16[2,48,2048]{2,1,0:T(8,128)(2,1)S(1)}, u32[]{:S(2)}, u32[]{:S(2)}) collective-permute-start(bf16[2,48,2048]{2,1,0:T(8,128)(2,1)S(1)} %pad_maximum_fusion.10), channel_id=1, source_target_pairs={{0,8},{4,12},{8,0},{12,4},{16,24},{20,28},{24,16},{28,20},{1,9},{5... | collective-permute-start | bytes 1179656 | tf_op jit(solution)/shard_map/ppermute | solution.py:154
  139.3 5.1 %collective-permute-start.18 = (bf16[4,48,2048]{2,1,0:T(8,128)(2,1)S(1)}, bf16[4,48,2048]{2,1,0:T(8,128)(2,1)S(1)}, u32[]{:S(2)}, u32[]{:S(2)}) collective-permute-start(bf16[4,48,2048]{2,1,0:T(8,128)(2,1)S(1)} %pad_maximum_fusion.4), channel_id=1, source_target_pairs={{0,4},{4,0},{8,12},{12,8},{16,20},{20,16},{24,28},{28,24},{1,5},{5... | collective-permute-start | bytes 2359304 | tf_op jit(solution)/shard_map/ppermute | solution.py:154
  139.4 5.1 %collective-permute-start.21 = (bf16[4,48,2048]{2,1,0:T(8,128)(2,1)S(1)}, bf16[4,48,2048]{2,1,0:T(8,128)(2,1)S(1)}, u32[]{:S(2)}, u32[]{:S(2)}) collective-permute-start(bf16[4,48,2048]{2,1,0:T(8,128)(2,1)S(1)} %pad_maximum_fusion.5), channel_id=1, source_target_pairs={{0,4},{4,0},{8,12},{12,8},{16,20},{20,16},{24,28},{28,24},{1,5},{5... | collective-permute-start | bytes 2359304 | tf_op jit(solution)/shard_map/ppermute | solution.py:154
  143.5 16.9 %collective-permute-start.6 = (bf16[4,48,2048]{2,1,0:T(8,128)(2,1)S(1)}, bf16[4,48,2048]{2,1,0:T(8,128)(2,1)S(1)}, u32[]{:S(2)}, u32[]{:S(2)}) collective-permute-start(bf16[4,48,2048]{2,1,0:T(8,128)(2,1)S(1)} %pad_maximum_fusion.2), channel_id=1, source_target_pairs={{0,4},{4,0},{8,12},{12,8},{16,20},{20,16},{24,28},{28,24},{1,5},{5... | collective-permute-start | bytes 2359304 | tf_op jit(solution)/shard_map/ppermute | solution.py:154
  143.7 16.9 %collective-permute-start.9 = (bf16[4,48,2048]{2,1,0:T(8,128)(2,1)S(1)}, bf16[4,48,2048]{2,1,0:T(8,128)(2,1)S(1)}, u32[]{:S(2)}, u32[]{:S(2)}) collective-permute-start(bf16[4,48,2048]{2,1,0:T(8,128)(2,1)S(1)} %pad_maximum_fusion.3), channel_id=1, source_target_pairs={{0,4},{4,0},{8,12},{12,8},{16,20},{20,16},{24,28},{28,24},{1,5},{5... | collective-permute-start | bytes 2359304 | tf_op jit(solution)/shard_map/ppermute | solution.py:154
  144.5 9.7 %slice-start.3 = ((s8[5767168]{0:T(1024)(128)(4,1)}), s8[4194304]{0:T(1024)(128)(4,1)S(1)}, s32[]{:S(2)}) async-start(s8[5767168]{0:T(1024)(128)(4,1)} %bitcast.124), calls=%async_computation.7 | async-start | bytes 8388608
  144.6 9.6 %slice-start.4 = ((s8[5767168]{0:T(1024)(128)(4,1)}), s8[1572864]{0:T(1024)(128)(4,1)S(1)}, s32[]{:S(2)}) async-start(s8[5767168]{0:T(1024)(128)(4,1)} %bitcast.124), calls=%async_computation.8 | async-start | bytes 3145728
  144.6 16.1 %slice-start = ((s8[11534336]{0:T(1024)(128)(4,1)}), s8[4194304]{0:T(1024)(128)(4,1)S(1)}, s32[]{:S(2)}) async-start(s8[11534336]{0:T(1024)(128)(4,1)} %bitcast.122), calls=%async_computation.4 | async-start | bytes 8388608
  144.6 16.1 %slice-start.1 = ((s8[11534336]{0:T(1024)(128)(4,1)}), s8[4194304]{0:T(1024)(128)(4,1)S(1)}, s32[]{:S(2)}) async-start(s8[11534336]{0:T(1024)(128)(4,1)} %bitcast.122), calls=%async_computation.5 | async-start | bytes 8388608
  154.2 6.6 %slice-start.2 = ((s8[11534336]{0:T(1024)(128)(4,1)}), s8[3145728]{0:T(1024)(128)(4,1)S(1)}, s32[]{:S(2)}) async-start(s8[11534336]{0:T(1024)(128)(4,1)} %bitcast.122), calls=%async_computation.6 | async-start | bytes 6291456
  159.9 13.5 %collective-permute-start.25 = (bf16[4,48,2048]{2,1,0:T(8,128)(2,1)S(1)}, bf16[4,48,2048]{2,1,0:T(8,128)(2,1)S(1)}, u32[]{:S(2)}, u32[]{:S(2)}) collective-permute-start(bf16[4,48,2048]{2,1,0:T(8,128)(2,1)S(1)} %bitcast.116), channel_id=1, source_target_pairs={{0,4},{4,0},{8,12},{12,8},{16,20},{20,16},{24,28},{28,24},{1,5},{5... | collective-permute-start | bytes 2359304 | tf_op jit(solution)/shard_map/ppermute | solution.py:154
  160.0 14.3 %collective-permute-start.22 = (bf16[4,48,2048]{2,1,0:T(8,128)(2,1)S(1)}, bf16[4,48,2048]{2,1,0:T(8,128)(2,1)S(1)}, u32[]{:S(2)}, u32[]{:S(2)}) collective-permute-start(bf16[4,48,2048]{2,1,0:T(8,128)(2,1)S(1)} %bitcast.115), channel_id=1, source_target_pairs={{0,4},{4,0},{8,12},{12,8},{16,20},{20,16},{24,28},{28,24},{1,5},{5... | collective-permute-start | bytes 2359304 | tf_op jit(solution)/shard_map/ppermute | solution.py:154
  172.8 3.4 %collective-permute-start.13 = (bf16[4,48,2048]{2,1,0:T(8,128)(2,1)S(1)}, bf16[4,48,2048]{2,1,0:T(8,128)(2,1)S(1)}, u32[]{:S(2)}, u32[]{:S(2)}) collective-permute-start(bf16[4,48,2048]{2,1,0:T(8,128)(2,1)S(1)} %bitcast.118), channel_id=1, source_target_pairs={{0,4},{4,0},{8,12},{12,8},{16,20},{20,16},{24,28},{28,24},{1,5},{5... | collective-permute-start | bytes 2359304 | tf_op jit(solution)/shard_map/ppermute | solution.py:154
  173.0 5.1 %collective-permute-start.10 = (bf16[4,48,2048]{2,1,0:T(8,128)(2,1)S(1)}, bf16[4,48,2048]{2,1,0:T(8,128)(2,1)S(1)}, u32[]{:S(2)}, u32[]{:S(2)}) collective-permute-start(bf16[4,48,2048]{2,1,0:T(8,128)(2,1)S(1)} %bitcast.117), channel_id=1, source_target_pairs={{0,4},{4,0},{8,12},{12,8},{16,20},{20,16},{24,28},{28,24},{1,5},{5... | collective-permute-start | bytes 2359304 | tf_op jit(solution)/shard_map/ppermute | solution.py:154
  173.7 12.0 %collective-permute-start.26 = (bf16[2,48,2048]{2,1,0:T(8,128)(2,1)S(1)}, bf16[2,48,2048]{2,1,0:T(8,128)(2,1)S(1)}, u32[]{:S(2)}, u32[]{:S(2)}) collective-permute-start(bf16[2,48,2048]{2,1,0:T(8,128)(2,1)S(1)} %slice.269), channel_id=1, source_target_pairs={{0,8},{4,12},{8,0},{12,4},{16,24},{20,28},{24,16},{28,20},{1,9},{5... | collective-permute-start | bytes 1179656 | tf_op jit(solution)/shard_map/ppermute | solution.py:154
  174.6 12.8 %collective-permute-start.23 = (bf16[2,48,2048]{2,1,0:T(8,128)(2,1)S(1)}, bf16[2,48,2048]{2,1,0:T(8,128)(2,1)S(1)}, u32[]{:S(2)}, u32[]{:S(2)}) collective-permute-start(bf16[2,48,2048]{2,1,0:T(8,128)(2,1)S(1)} %slice.263), channel_id=1, source_target_pairs={{0,16},{4,20},{8,24},{12,28},{16,0},{20,4},{24,8},{28,12},{1,17},{... | collective-permute-start | bytes 1179656 | tf_op jit(solution)/shard_map/ppermute | solution.py:154
  176.5 17.6 %collective-permute-start.14 = (bf16[2,48,2048]{2,1,0:T(8,128)(2,1)S(1)}, bf16[2,48,2048]{2,1,0:T(8,128)(2,1)S(1)}, u32[]{:S(2)}, u32[]{:S(2)}) collective-permute-start(bf16[2,48,2048]{2,1,0:T(8,128)(2,1)S(1)} %slice.252), channel_id=1, source_target_pairs={{0,8},{4,12},{8,0},{12,4},{16,24},{20,28},{24,16},{28,20},{1,9},{5... | collective-permute-start | bytes 1179656 | tf_op jit(solution)/shard_map/ppermute | solution.py:154
  178.4 17.5 %collective-permute-start.11 = (bf16[2,48,2048]{2,1,0:T(8,128)(2,1)S(1)}, bf16[2,48,2048]{2,1,0:T(8,128)(2,1)S(1)}, u32[]{:S(2)}, u32[]{:S(2)}) collective-permute-start(bf16[2,48,2048]{2,1,0:T(8,128)(2,1)S(1)} %slice.246), channel_id=1, source_target_pairs={{0,16},{4,20},{8,24},{12,28},{16,0},{20,4},{24,8},{28,12},{1,17},{... | collective-permute-start | bytes 1179656 | tf_op jit(solution)/shard_map/ppermute | solution.py:154
  185.9 13.5 %collective-permute-start.27 = (bf16[1,48,2048]{2,1,0:T(8,128)(2,1)S(1)}, bf16[1,48,2048]{2,1,0:T(8,128)(2,1)S(1)}, u32[]{:S(2)}, u32[]{:S(2)}) collective-permute-start(bf16[1,48,2048]{2,1,0:T(8,128)(2,1)S(1)} %slice.271), channel_id=1, source_target_pairs={{0,16},{4,20},{8,24},{12,28},{16,0},{20,4},{24,8},{28,12},{1,17},{... | collective-permute-start | bytes 589832 | tf_op jit(solution)/shard_map/ppermute | solution.py:154
  187.6 11.8 %collective-permute-start.24 = (bf16[1,48,2048]{2,1,0:T(8,128)(2,1)S(1)}, bf16[1,48,2048]{2,1,0:T(8,128)(2,1)S(1)}, u32[]{:S(2)}, u32[]{:S(2)}) collective-permute-start(bf16[1,48,2048]{2,1,0:T(8,128)(2,1)S(1)} %slice.265), channel_id=1, source_target_pairs={{0,8},{4,12},{8,0},{12,4},{16,24},{20,28},{24,16},{28,20},{1,9},{5... | collective-permute-start | bytes 589832 | tf_op jit(solution)/shard_map/ppermute | solution.py:154
  194.3 10.3 %collective-permute-start.15 = (bf16[1,48,2048]{2,1,0:T(8,128)(2,1)S(1)}, bf16[1,48,2048]{2,1,0:T(8,128)(2,1)S(1)}, u32[]{:S(2)}, u32[]{:S(2)}) collective-permute-start(bf16[1,48,2048]{2,1,0:T(8,128)(2,1)S(1)} %slice.254), channel_id=1, source_target_pairs={{0,16},{4,20},{8,24},{12,28},{16,0},{20,4},{24,8},{28,12},{1,17},{... | collective-permute-start | bytes 589832 | tf_op jit(solution)/shard_map/ppermute | solution.py:154
  196.0 8.7 %collective-permute-start.12 = (bf16[1,48,2048]{2,1,0:T(8,128)(2,1)S(1)}, bf16[1,48,2048]{2,1,0:T(8,128)(2,1)S(1)}, u32[]{:S(2)}, u32[]{:S(2)}) collective-permute-start(bf16[1,48,2048]{2,1,0:T(8,128)(2,1)S(1)} %slice.248), channel_id=1, source_target_pairs={{0,8},{4,12},{8,0},{12,4},{16,24},{20,28},{24,16},{28,20},{1,9},{5... | collective-permute-start | bytes 589832 | tf_op jit(solution)/shard_map/ppermute | solution.py:154
  200.3 28.3 %copy-start.1 = (f32[2048,8]{0,1:T(8,128)S(1)}, f32[2048,8]{0,1:T(8,128)}, u32[]{:S(2)}) copy-start(f32[2048,8]{0,1:T(8,128)} %param.20) | copy-start | bytes 196612
  200.3 14.0 %all-to-all-start.3 = ((bf16[4,24,2048]{2,1,0:T(8,128)(2,1)}), bf16[4,24,2048]{2,1,0:T(8,128)(2,1)S(1)}, u32[]{:S(2)}, u32[]{:S(2)}) async-start(bf16[4,24,2048]{2,1,0:T(8,128)(2,1)} %bitcast.38), calls=%async_computation.3 | async-start | bytes 786432 | tf_op jit(solution)/shard_map/all_to_all | solution.py:278
  214.3 13.0 %all-to-all-start.1 = ((bf16[4,24,2048]{2,1,0:T(8,128)(2,1)}), bf16[4,24,2048]{2,1,0:T(8,128)(2,1)S(1)}, u32[]{:S(2)}, u32[]{:S(2)}) async-start(bf16[4,24,2048]{2,1,0:T(8,128)(2,1)} %bitcast.24), calls=%async_computation.1 | async-start | bytes 786432 | tf_op jit(solution)/shard_map/all_to_all | solution.py:278
